TPU v7x, 32 devices: a whole 2x2x4 slice. The times are simulated.
32 devices in a mesh: seq: 8 (over y, x, core), fsdp: 4 (over z).
Axes of the slice: x: 2, y: 2, z: 4, core: 2. Of those that a mesh axis runs over, the one named last changes fastest.
Arguments:
- features: bfloat16 [16384, 1280], P(('seq', 'fsdp')), may hold values from -40 to 40
- conv_weight: bfloat16 [5, 1280, 1536], P(None, None, 'fsdp'), may hold values from -0.078125 to 0.078125
- mix_weight: bfloat16 [1536, 1536], P(None, 'fsdp'), may hold values from -0.15625 to 0.15625
- pool_weight: bfloat16 [1536, 1536], P(None, 'fsdp'), may hold values from -0.21875 to 0.21875
- gain_first: bfloat16 [1280], P('fsdp'), may hold values from 0.099609375 to 1.8984375
- shift_first: bfloat16 [1280], P('fsdp'), may hold values from -3 to 3
- gain_second: bfloat16 [1536], P('fsdp'), may hold values from 0.099609375 to 1.8984375
- shift_second: bfloat16 [1536], P('fsdp'), may hold values from -3 to 3
- bias_conv: bfloat16 [1536], P('fsdp'), may hold values from -3 to 3
- bias_mix: bfloat16 [1536], P('fsdp'), may hold values from -3 to 3
- cotangent: bfloat16 [8192, 1536], P(('seq', 'fsdp')), may hold values from -6 to 6
- track_counts: int32 [8], replicated, may hold values from 1 to 5313, as said below
Outputs:
- pooled: bfloat16 [8192, 1536], P(('seq', 'fsdp'))
- grad_features: bfloat16 [16384, 1280], P(('seq', 'fsdp'))
- grad_conv: float32 [5, 1280, 1536], P(None, None, 'fsdp')
- grad_mix: float32 [1536, 1536], P(None, 'fsdp')
- grad_pool: float32 [1536, 1536], P(None, 'fsdp')
- grad_gain_first: float32 [1280], P('fsdp')
- grad_shift_first: float32 [1280], P('fsdp')
- grad_gain_second: float32 [1536], P('fsdp')
- grad_shift_second: float32 [1536], P('fsdp')
- grad_bias_conv: float32 [1536], P('fsdp')
- grad_bias_mix: float32 [1536], P('fsdp')
Inputs may be any that keep to these rules, and one draw needn't show every extreme that they name: `track_counts`: each window has between 1 and 5313 present tracks; some window has 5313 and some other window has 1.
All inputs are finite; a program needn't handle non-finite values.
Results may differ from a plain program's by a relative error of at most 0.015.
Values may be sent and summed in bfloat16 or wider, within the bound.
A program may use at most 256 MiB of HBM per device.

v0:
```python
import jax
import jax.numpy as jnp
from jax import lax
from jax.sharding import PartitionSpec as P

TRACKS = 5313
WIN = 2048


epsilon = 1e-05


def extended(shard, sides, width):
    for axis, dim in sides:
        size, length = (lax.axis_size(axis), shard.shape[dim])
        up = [(i, (i + 1) % size) for i in range(size - 1)]
        down = [(j, i) for i, j in up]
        last = lax.slice_in_dim(shard, length - width, length, axis=dim)
        first = lax.slice_in_dim(shard, 0, width, axis=dim)
        before = lax.ppermute(last, axis, up)
        after = lax.ppermute(first, axis, down)
        shard = jnp.concatenate([before, shard, after], axis=dim)
    return shard


def activate(values):
    return jax.nn.gelu(values, approximate=False)


def activate_back(before, grad_after):
    unused, pull = jax.vjp(activate, before)
    return pull(grad_after)[0]


def pair_softmax(logits):
    pair_max = jnp.max(logits, axis=1, keepdims=True)
    exponent = jnp.exp(logits - pair_max)
    return exponent / jnp.sum(exponent, axis=1, keepdims=True)


def sharded_path(
    features,
    conv_weight,
    mix_weight,
    pool_weight,
    gain_first,
    shift_first,
    gain_second,
    shift_second,
    bias_conv,
    bias_mix,
    cotangent,
    track_scale,
    normed_one,
    total_rows,
):
    row_count = features.shape[0]
    width_count = conv_weight.shape[0]
    half_width = (width_count - 1) // 2
    gathered = (
        lax.all_gather(conv_weight, "fsdp", axis=2, tiled=True),
        lax.all_gather(mix_weight, "fsdp", axis=1, tiled=True),
        lax.all_gather(pool_weight, "fsdp", axis=1, tiled=True),
        lax.all_gather(gain_first, "fsdp", axis=0, tiled=True),
        lax.all_gather(shift_first, "fsdp", axis=0, tiled=True),
        lax.all_gather(gain_second, "fsdp", axis=0, tiled=True),
        lax.all_gather(shift_second, "fsdp", axis=0, tiled=True),
        lax.all_gather(bias_conv, "fsdp", axis=0, tiled=True),
        lax.all_gather(bias_mix, "fsdp", axis=0, tiled=True),
    )
    full_conv, full_mix, full_pool = (gathered[0], gathered[1], gathered[2])
    gain_one, shift_one, gain_two, shift_two, bias_one, bias_two = [
        item.astype(jnp.float32) for item in gathered[3:]
    ]
    before_one = normed_one * gain_one + shift_one
    active_one = activate(before_one).astype(jnp.bfloat16)
    padded_one = extended(active_one, (("fsdp", 0),), 2)
    conv_out = jnp.dot(padded_one[0:row_count], full_conv[0], preferred_element_type=jnp.float32)
    for offset in range(1, width_count):
        conv_out = conv_out + jnp.dot(
            padded_one[offset : offset + row_count],
            full_conv[offset],
            preferred_element_type=jnp.float32,
        )
    middle = conv_out + bias_one
    center_two = lax.psum(jnp.sum(middle, axis=0), ("seq", "fsdp")) / total_rows
    spread_two = (
        lax.psum(jnp.sum(jnp.square(middle - center_two), axis=0), ("seq", "fsdp")) / total_rows
    )
    scale_two = lax.rsqrt(spread_two + epsilon)
    normed_two = (middle - center_two) * scale_two
    before_two = normed_two * gain_two + shift_two
    active_two = activate(before_two).astype(jnp.bfloat16)
    summed = middle + jnp.dot(active_two, full_mix, preferred_element_type=jnp.float32) + bias_two
    summed_low = summed.astype(jnp.bfloat16)
    logits = jnp.dot(summed_low, full_pool, preferred_element_type=jnp.float32).reshape(
        row_count // 2, 2, -1
    )
    weights = pair_softmax(logits)
    pair_values = summed.reshape(row_count // 2, 2, -1)
    pooled = jnp.sum(weights * pair_values, axis=1).astype(jnp.bfloat16)
    upstream = cotangent.astype(jnp.float32) * track_scale
    grad_pairs = weights * upstream[:, None, :]
    spread_grad = pair_values * upstream[:, None, :]
    grad_logits = weights * (spread_grad - jnp.sum(weights * spread_grad, axis=1, keepdims=True))
    logit_low = grad_logits.reshape(row_count, -1).astype(jnp.bfloat16)
    back_conv, back_mix, back_pool = (
        lax.all_gather(conv_weight, "fsdp", axis=2, tiled=True),
        lax.all_gather(mix_weight, "fsdp", axis=1, tiled=True),
        lax.all_gather(pool_weight, "fsdp", axis=1, tiled=True),
    )
    term_pool = jnp.einsum("pc,pd->cd", summed_low, logit_low, preferred_element_type=jnp.float32)
    grad_summed = grad_pairs.reshape(row_count, -1) + jnp.einsum(
        "pd,cd->pc", logit_low, back_pool, preferred_element_type=jnp.float32
    )
    term_bias_two = jnp.sum(grad_summed, axis=0)
    branch_low = grad_summed.astype(jnp.bfloat16)
    term_mix = jnp.einsum("pc,pd->cd", active_two, branch_low, preferred_element_type=jnp.float32)
    grad_active_two = jnp.einsum(
        "pd,cd->pc", branch_low, back_mix, preferred_element_type=jnp.float32
    )
    grad_before_two = activate_back(before_two, grad_active_two)
    shift_two_grad, gain_two_grad = lax.psum(
        (jnp.sum(grad_before_two, axis=0), jnp.sum(grad_before_two * normed_two, axis=0)),
        ("seq", "fsdp"),
    )
    grad_middle = grad_summed + gain_two * scale_two * (
        grad_before_two - shift_two_grad / total_rows - normed_two * gain_two_grad / total_rows
    )
    term_bias_one = jnp.sum(grad_middle, axis=0)
    middle_low = grad_middle.astype(jnp.bfloat16)
    term_conv = jnp.stack(
        [
            jnp.einsum(
                "pc,pd->cd",
                padded_one[offset : offset + row_count],
                middle_low,
                preferred_element_type=jnp.float32,
            )
            for offset in range(width_count)
        ]
    )
    padded_grad = extended(middle_low, (("fsdp", 0),), 2)
    grad_active_one = jnp.einsum(
        "pd,cd->pc",
        padded_grad[2 * half_width : 2 * half_width + row_count],
        back_conv[0],
        preferred_element_type=jnp.float32,
    )
    for offset in range(1, width_count):
        begin = 2 * half_width - offset
        grad_active_one = grad_active_one + jnp.einsum(
            "pd,cd->pc",
            padded_grad[begin : begin + row_count],
            back_conv[offset],
            preferred_element_type=jnp.float32,
        )
    partial_grads = (
        lax.psum_scatter(
            term_conv.astype(jnp.bfloat16), "fsdp", scatter_dimension=2, tiled=True
        ).astype(jnp.float32),
        lax.psum_scatter(
            term_mix.astype(jnp.bfloat16), "fsdp", scatter_dimension=1, tiled=True
        ).astype(jnp.float32),
        lax.psum_scatter(
            term_pool.astype(jnp.bfloat16), "fsdp", scatter_dimension=1, tiled=True
        ).astype(jnp.float32),
        lax.psum_scatter(
            term_bias_one.astype(jnp.bfloat16), "fsdp", scatter_dimension=0, tiled=True
        ).astype(jnp.float32),
        lax.psum_scatter(
            term_bias_two.astype(jnp.bfloat16), "fsdp", scatter_dimension=0, tiled=True
        ).astype(jnp.float32),
    )
    grad_conv, grad_mix, grad_pool, grad_bias_conv, grad_bias_mix = lax.psum(
        (partial_grads[0], partial_grads[1], partial_grads[2], partial_grads[3], partial_grads[4]),
        "seq",
    )
    owner = lax.axis_index("fsdp")
    second_share = gain_second.shape[0]
    grad_gain_second = lax.dynamic_slice_in_dim(gain_two_grad, owner * second_share, second_share)
    grad_shift_second = lax.dynamic_slice_in_dim(shift_two_grad, owner * second_share, second_share)
    return (
        pooled,
        grad_active_one,
        gain_one,
        before_one,
        grad_conv,
        grad_mix,
        grad_pool,
        grad_gain_second,
        grad_shift_second,
        grad_bias_conv,
        grad_bias_mix,
    )


def on_device(
    features,
    conv_weight,
    mix_weight,
    pool_weight,
    gain_first,
    shift_first,
    gain_second,
    shift_second,
    bias_conv,
    bias_mix,
    cotangent,
    track_counts,
):
    row_count = features.shape[0]
    total_rows = float(row_count * lax.axis_size(("seq", "fsdp")))
    position = lax.axis_index(("seq", "fsdp"))
    window = position * row_count // WIN
    track_scale = lax.dynamic_slice_in_dim(track_counts, window, 1).astype(jnp.float32) / TRACKS
    inputs = features.astype(jnp.float32)
    center_one = lax.psum(jnp.sum(inputs, axis=0), ("seq", "fsdp")) / total_rows
    spread_one = (
        lax.psum(jnp.sum(jnp.square(inputs - center_one), axis=0), ("seq", "fsdp")) / total_rows
    )
    scale_one = lax.rsqrt(spread_one + epsilon)
    normed_one = (inputs - center_one) * scale_one
    results = sharded_path(
        features,
        conv_weight,
        mix_weight,
        pool_weight,
        gain_first,
        shift_first,
        gain_second,
        shift_second,
        bias_conv,
        bias_mix,
        cotangent,
        track_scale,
        normed_one,
        total_rows,
    )
    (
        pooled,
        grad_active_one,
        gain_one,
        before_one,
        grad_conv,
        grad_mix,
        grad_pool,
        grad_gain_second,
        grad_shift_second,
        grad_bias_conv,
        grad_bias_mix,
    ) = results
    grad_before_one = activate_back(before_one, grad_active_one)
    shift_one_grad, gain_one_grad = lax.psum(
        (jnp.sum(grad_before_one, axis=0), jnp.sum(grad_before_one * normed_one, axis=0)),
        ("seq", "fsdp"),
    )
    grad_features = (
        gain_one
        * scale_one
        * (grad_before_one - shift_one_grad / total_rows - normed_one * gain_one_grad / total_rows)
    ).astype(jnp.bfloat16)
    owner = lax.axis_index("fsdp")
    first_share = gain_first.shape[0]
    grad_gain_first = lax.dynamic_slice_in_dim(gain_one_grad, owner * first_share, first_share)
    grad_shift_first = lax.dynamic_slice_in_dim(shift_one_grad, owner * first_share, first_share)
    return (
        pooled,
        grad_features,
        grad_conv,
        grad_mix,
        grad_pool,
        grad_gain_first,
        grad_shift_first,
        grad_gain_second,
        grad_shift_second,
        grad_bias_conv,
        grad_bias_mix,
    )


def solution(mesh):
    in_specs = (
        P(("seq", "fsdp"), None),
        P(None, None, "fsdp"),
        P(None, "fsdp"),
        P(None, "fsdp"),
        P("fsdp"),
        P("fsdp"),
        P("fsdp"),
        P("fsdp"),
        P("fsdp"),
        P("fsdp"),
        P(("seq", "fsdp"), None),
        P(),
    )
    out_specs = (
        P(("seq", "fsdp"), None),
        P(("seq", "fsdp"), None),
        P(None, None, "fsdp"),
        P(None, "fsdp"),
        P(None, "fsdp"),
        P("fsdp"),
        P("fsdp"),
        P("fsdp"),
        P("fsdp"),
        P("fsdp"),
        P("fsdp"),
    )
    return jax.shard_map(
        on_device, mesh=mesh, in_specs=in_specs, out_specs=out_specs, check_vma=False
    )
```

profile of v0, /device:TPU:0, one launch (start us, length us, event | category | flops | bytes accessed | tf_op | source)
XLA Modules:
  0.0 1425.1 jit_solution(14680301219492304652)
XLA Ops:
  10.5 13.7 all-reduce.8
  24.5 54.5 %psum.91 = f32[1280]{0:T(1024)S(1)} all-reduce(f32[1280]{0:T(1024)S(1)} %convert_reduce_fusion), channel_id=1, replica_groups=mesh['seq'=8,'fsdp'=4] {'seq','fsdp'}, use_global_device_ids=true, to_apply=%region_1.2 | all-reduce | flops 1280 | bytes 10240 | tf_op jit(solution)/shard_map/psum | solution.py:218
  79.5 52.0 %psum.92 = f32[1280]{0:T(1024)S(1)} all-reduce(f32[1280]{0:T(1024)S(1)} %fusion.52), channel_id=1, replica_groups=mesh['seq'=8,'fsdp'=4] {'seq','fsdp'}, use_global_device_ids=true, to_apply=%region_3.4 | all-reduce | flops 1280 | bytes 10240 | tf_op jit(solution)/shard_map/psum | solution.py:220
  132.1 6.2 multiply_convert_fusion.2
  143.4 20.1 %all-gather.3 = bf16[4,1,384]{2,1,0:T(2,128)(2,1)S(1)} all-gather(bf16[1,1,384]{2,1,0:T(2,128)(2,1)S(1)} %reshape.72), channel_id=1, replica_groups=mesh['seq'=8,'fsdp'=4] {'fsdp'}, dimensions={0}, use_global_device_ids=true | all-gather | bytes 3840 | tf_op jit(solution)/shard_map/all_gather | solution.py:69
  163.5 14.1 all-gather
  177.7 36.8 %all-gather.2 = bf16[4,1,384]{2,1,0:T(2,128)(2,1)S(1)} all-gather(bf16[1,1,384]{2,1,0:T(2,128)(2,1)S(1)} %reshape.70), channel_id=1, replica_groups=mesh['seq'=8,'fsdp'=4] {'fsdp'}, dimensions={0}, use_global_device_ids=true | all-gather | bytes 3840 | tf_op jit(solution)/shard_map/all_gather | solution.py:67
  214.5 15.0 %all-gather.1 = bf16[4,1,384]{2,1,0:T(2,128)(2,1)S(1)} all-gather(bf16[1,1,384]{2,1,0:T(2,128)(2,1)S(1)} %reshape.68), channel_id=1, replica_groups=mesh['seq'=8,'fsdp'=4] {'fsdp'}, dimensions={0}, use_global_device_ids=true | all-gather | bytes 3840 | tf_op jit(solution)/shard_map/all_gather | solution.py:66
  236.7 113.7 %all-gather.8.cloned.1.call-done = bf16[5,1280,1536]{2,1,0:T(8,128)(2,1)} async-done(((bf16[5,1280,384]{2,1,0:T(8,128)(2,1)}), bf16[5,1280,1536]{2,1,0:T(8,128)(2,1)}) %all-gather.8.cloned.1.call-update) | async-done | bytes 19660816 | tf_op jit(solution)/shard_map/all_gather | solution.py:61
  350.5 6.5 fusion.20
  357.0 5.7 fusion.14
  367.2 4.3 fusion.99
  371.5 45.8 %psum.93 = f32[1536]{0:T(1024)S(1)} all-reduce(f32[1536]{0:T(1024)S(1)} %get-tuple-element.43), channel_id=1, replica_groups=mesh['seq'=8,'fsdp'=4] {'seq','fsdp'}, use_global_device_ids=true, to_apply=%region_5.6 | all-reduce | flops 1536 | bytes 12288 | tf_op jit(solution)/shard_map/psum | solution.py:86
  417.7 40.9 %psum.94 = f32[1536]{0:T(1024)S(1)} all-reduce(f32[1536]{0:T(1024)S(1)} %multiply_reduce_fusion.3), channel_id=1, replica_groups=mesh['seq'=8,'fsdp'=4] {'seq','fsdp'}, use_global_device_ids=true, to_apply=%region_7.8 | all-reduce | flops 1536 | bytes 12288 | tf_op jit(solution)/shard_map/psum | solution.py:88
  458.6 7.8 fusion.31
  466.4 7.8 fusion.30
  477.3 54.0 %all-gather.12.cloned.1.call-done = bf16[1536,1536]{1,0:T(8,128)(2,1)} async-done(((bf16[1536,384]{1,0:T(8,128)(2,1)}), bf16[1536,1536]{1,0:T(8,128)(2,1)}) %all-gather.12.cloned.1.call-update) | async-done | bytes 4718608 | tf_op jit(solution)/shard_map/all_gather | solution.py:63
  531.2 6.6 fusion.77
  541.8 5.4 reduce_max.9
  547.2 6.6 fusion.61
  553.8 7.8 multiply_reduce_fusion.2
  561.6 4.9 fusion
  566.5 5.7 sub.85
  574.9 5.4 sub.81
  583.1 5.4 div.61
  588.5 10.5 convolution_convert_fusion
  599.0 6.7 copy.27
  606.0 16.6 %convolution_add_fusion = f32[512,1536]{1,0:T(8,128)} fusion(bf16[1536,1536]{1,0:T(8,128)(2,1)} %all-gather.12.cloned.1.call-done, f32[512,1536]{1,0:T(8,128)} %mul.217, f32[512,1536]{1,0:T(8,128)} %div.61, f32[512,1536]{1,0:T(8,128)} %fusion.77, f32[512,1536]{1,0:T(8,128)} %sub.81, f32[512,1536]{1,0:T(8,128)} %sub.85, f32[512,1536]{1,0:T(8,128)S(1)} %copy-done.1), kind=kOutput, calls=%fused_computation.46 | convolution fusion | flops 2423783424 | bytes 26738688 | tf_op jit(solution)/shard_map/pd,cd->pc/dot_general | solution.py:113
  622.5 7.8 convolution_convert_fusion.1
  630.3 6.7 copy.25
  638.9 9.9 fusion.92
  648.8 44.5 %all-reduce.5 = (f32[1536]{0:T(1024)S(1)}, f32[1536]{0:T(1024)S(1)}) all-reduce(f32[1536]{0:T(1024)S(1)} %get-tuple-element.12, f32[1536]{0:T(1024)S(1)} %get-tuple-element.11), channel_id=1, replica_groups=mesh['seq'=8,'fsdp'=4] {'seq','fsdp'}, use_global_device_ids=true, to_apply=%region_15.16 | all-reduce | flops 3072 | bytes 24576 | tf_op jit(solution)/shard_map/psum | solution.py:123
  693.3 4.2 fusion.94
  697.5 4.2 fusion.2
  718.3 37.3 %copy.23 = bf16[5,1280,1536]{1,0,2:T(8,128)(2,1)} copy(bf16[5,1280,1536]{2,1,0:T(8,128)(2,1)} %fusion.10) | data formatting | bytes 39321600
  755.6 22.6 %copy.29 = bf16[192,8,5,1280]{3,1,2,0:T(8,128)(2,1)} copy(bf16[192,8,5,1280]{3,2,1,0:T(8,128)(2,1)} %bitcast.87) | data formatting | bytes 39321600
  781.7 4.5 collective-permute-start.3
  786.2 11.3 all-reduce.7
  797.6 4.4 fusion.15
  802.0 4.4 fusion.19
  806.4 4.4 fusion.13
  810.8 4.5 fusion.23
  815.4 12.6 fusion.93
  828.0 45.2 %all-reduce.4 = (f32[1280]{0:T(1024)S(1)}, f32[1280]{0:T(1024)S(1)}) all-reduce(f32[1280]{0:T(1024)S(1)} %get-tuple-element.14, f32[1280]{0:T(1024)S(1)} %get-tuple-element.13), channel_id=1, replica_groups=mesh['seq'=8,'fsdp'=4] {'seq','fsdp'}, use_global_device_ids=true, to_apply=%region_19.20 | all-reduce | flops 2560 | bytes 20480 | tf_op jit(solution)/shard_map/psum | solution.py:254
  881.4 227.6 %reduce-scatter.10.cloned.1.call-done = bf16[384,6400]{1,0:T(8,128)(2,1)} async-done(((bf16[1536,6400]{1,0:T(8,128)(2,1)}), bf16[384,6400]{1,0:T(8,128)(2,1)}) %reduce-scatter.10.cloned.1.call-update) | async-done | bytes 4915216
  1109.0 11.9 reshape.83
  1120.9 9.7 copy.24
  1130.6 287.4 %all-reduce.10 = (f32[5,1280,384]{2,1,0:T(8,128)}, f32[1536,384]{1,0:T(8,128)}, f32[1536,384]{1,0:T(8,128)}, f32[384]{0:T(512)}, f32[384]{0:T(512)}) all-reduce(bf16[5,1280,384]{2,1,0:T(8,128)(2,1)} %copy.24, bf16[1536,384]{1,0:T(8,128)(2,1)S(1)} %copy.26, ...), channel_id=1, replica_groups=mesh['seq'=8,'fsdp'=4] {'seq'}, use_global_device_ids=true, to_apply=%region_21.22 | all-reduce | flops 3638016 | bytes 21829632 | tf_op jit(solution)/shard_map/psum | solution.py:175
  (150 shorter events, 62.5 us)
Async XLA Ops:
  7.2 1.6 copy-start.29
  7.2 2.8 copy-start.30
  7.2 3.1 copy-start.31
  7.2 17.1 %copy-start.7 = (bf16[512,1280]{1,0:T(8,128)(2,1)S(1)}, bf16[512,1280]{1,0:T(8,128)(2,1)}, u32[]{:S(2)}) copy-start(bf16[512,1280]{1,0:T(8,128)(2,1)} %param.12) | copy-start | bytes 3932164
  7.2 343.3 %all-gather.8.cloned.1.call-start = ((), (), s32[]{:S(2)}) async-start(), calls=%async_computation.3 | async-start | bytes 24576000 | tf_op jit(solution)/shard_map/all_gather | solution.py:61
  8.0 458.5 %all-gather.10.cloned.1.call-start = ((), (), s32[]{:S(2)}) async-start(), calls=%async_computation.4 | async-start | bytes 5898240 | tf_op jit(solution)/shard_map/all_gather | solution.py:62
  8.7 522.5 %all-gather.12.cloned.1.call-start = ((), (), s32[]{:S(2)}) async-start(), calls=%async_computation.5 | async-start | bytes 5898240 | tf_op jit(solution)/shard_map/all_gather | solution.py:63
  24.3 114.0 %copy-start.25 = (f32[1280]{0:T(1024)}, f32[1280]{0:T(1024)S(1)}, u32[]{:S(2)}) copy-start(f32[1280]{0:T(1024)S(1)} %convert_element_type.81) | copy-start | bytes 15364
  24.3 114.0 %copy-start.27 = (f32[1280]{0:T(1024)}, f32[1280]{0:T(1024)S(1)}, u32[]{:S(2)}) copy-start(f32[1280]{0:T(1024)S(1)} %convert_element_type.80) | copy-start | bytes 15364
  79.0 63.0 %copy-start.20 = (f32[1280]{0:T(1024)}, f32[1280]{0:T(1024)S(1)}, u32[]{:S(2)}) copy-start(f32[1280]{0:T(1024)S(1)} %broadcast_multiply_fusion.3) | copy-start | bytes 15364
  79.0 63.0 %copy-start.37 = (s32[8]{0:T(128)S(1)}, s32[8]{0:T(128)}, u32[]{:S(2)}) copy-start(s32[8]{0:T(128)} %param.23) | copy-start | bytes 100
  79.0 64.3 %copy-start.32 = (bf16[384]{0:T(512)(128)(2,1)S(1)}, bf16[384]{0:T(512)(128)(2,1)}, u32[]{:S(2)}) copy-start(bf16[384]{0:T(512)(128)(2,1)} %param.18) | copy-start | bytes 2308
  79.0 64.3 %copy-start.33 = (bf16[384]{0:T(512)(128)(2,1)S(1)}, bf16[384]{0:T(512)(128)(2,1)}, u32[]{:S(2)}) copy-start(bf16[384]{0:T(512)(128)(2,1)} %param.19) | copy-start | bytes 2308
  79.1 64.3 %copy-start.34 = (bf16[384]{0:T(512)(128)(2,1)S(1)}, bf16[384]{0:T(512)(128)(2,1)}, u32[]{:S(2)}) copy-start(bf16[384]{0:T(512)(128)(2,1)} %param.20) | copy-start | bytes 2308
  79.1 64.3 %copy-start.35 = (bf16[384]{0:T(512)(128)(2,1)S(1)}, bf16[384]{0:T(512)(128)(2,1)}, u32[]{:S(2)}) copy-start(bf16[384]{0:T(512)(128)(2,1)} %param.21) | copy-start | bytes 2308
  79.1 150.4 %copy-start.19 = (bf16[256,1536]{1,0:T(8,128)(2,1)S(1)}, bf16[256,1536]{1,0:T(8,128)(2,1)}, u32[]{:S(2)}) copy-start(bf16[256,1536]{1,0:T(8,128)(2,1)} %param.22) | copy-start | bytes 2359300
  132.1 7.3 copy-start.22
  138.3 1.1 copy-start.15
  139.4 217.7 %collective-permute-start = (bf16[2,1280]{1,0:T(2,128)(2,1)S(1)}, bf16[2,1280]{1,0:T(2,128)(2,1)S(1)}, u32[]{:S(2)}, u32[]{:S(2)}) collective-permute-start(bf16[2,1280]{1,0:T(2,128)(2,1)S(1)} %get-tuple-element.35), channel_id=1, source_target_pairs={{0,1},{1,2},{2,3},{4,5},{5,6},{6,7},{8,9},{9,10},{10,11},{12,13},{... | collective-permute-start | bytes 15368 | tf_op jit(solution)/shard_map/ppermute | solution.py:20
  140.6 96.1 %collective-permute-start.1 = (bf16[2,1280]{1,0:T(2,128)(2,1)S(1)}, bf16[2,1280]{1,0:T(2,128)(2,1)S(1)}, u32[]{:S(2)}, u32[]{:S(2)}) collective-permute-start(bf16[2,1280]{1,0:T(2,128)(2,1)S(1)} %get-tuple-element.36), channel_id=1, source_target_pairs={{1,0},{2,1},{3,2},{5,4},{6,5},{7,6},{9,8},{10,9},{11,10},{13,12},{... | collective-permute-start | bytes 15368 | tf_op jit(solution)/shard_map/ppermute | solution.py:21
  142.0 736.0 %reduce-scatter.14.cloned.1.call-start = ((), (), s32[]{:S(2)}) async-start(), calls=%async_computation.8 | async-start | bytes 5898240
  236.7 120.3 %copy-start.16 = (bf16[512,1280]{1,0:T(8,128)(2,1)S(1)}, bf16[512,1280]{1,0:T(8,128)(2,1)}, u32[]{:S(2)}) copy-start(bf16[512,1280]{1,0:T(8,128)(2,1)} %copy-done.15) | copy-start | bytes 3932164
  350.5 12.2 copy-start.36
  364.9 2.3 copy-start.17
  371.5 94.9 %copy-start.2 = (f32[512,1536]{1,0:T(8,128)}, f32[512,1536]{1,0:T(8,128)S(1)}, u32[]{:S(2)}) copy-start(f32[512,1536]{1,0:T(8,128)S(1)} %get-tuple-element.44) | copy-start | bytes 9437188
  474.2 57.0 %copy-start = (f32[512,1536]{1,0:T(8,128)}, f32[512,1536]{1,0:T(8,128)S(1)}, u32[]{:S(2)}) copy-start(f32[512,1536]{1,0:T(8,128)S(1)} %fusion.30) | copy-start | bytes 9437188
  547.1 6.6 copy-start.5
  547.2 6.6 copy-start.11
  553.8 7.8 copy-start.9
  553.8 7.8 copy-start.12
  566.5 5.7 copy-start.6
  574.9 5.4 copy-start.10
  583.1 5.4 copy-start.1
  605.7 274.0 %reduce-scatter.12.cloned.1.call-start = ((), (), s32[]{:S(2)}) async-start(), calls=%async_computation.7 | async-start | bytes 5898240
  605.9 16.6 %copy-start.3 = (f32[512,1536]{1,0:T(8,128)S(1)}, f32[512,1536]{1,0:T(8,128)}, u32[]{:S(2)}) copy-start(f32[512,1536]{1,0:T(8,128)} %copy-done.2) | copy-start | bytes 9437188
  637.0 1.9 copy-start.4
  637.0 472.0 %reduce-scatter.10.cloned.1.call-start = ((), (), s32[]{:S(2)}) async-start(), calls=%async_computation.6 | async-start | bytes 24576000
  693.3 4.2 copy-start.18
  697.5 16.6 %copy-start.13 = (bf16[512,1536]{1,0:T(8,128)(2,1)}, bf16[512,1536]{1,0:T(8,128)(2,1)S(1)}, u32[]{:S(2)}) copy-start(bf16[512,1536]{1,0:T(8,128)(2,1)S(1)} %get-tuple-element.29) | copy-start | bytes 4718596
  778.2 2.1 copy-start.14
  780.4 26.1 %collective-permute-start.2 = (bf16[2,1536]{1,0:T(2,128)(2,1)S(1)}, bf16[2,1536]{1,0:T(2,128)(2,1)S(1)}, u32[]{:S(2)}, u32[]{:S(2)}) collective-permute-start(bf16[2,1536]{1,0:T(2,128)(2,1)S(1)} %get-tuple-element.33), channel_id=1, source_target_pairs={{1,0},{2,1},{3,2},{5,4},{6,5},{7,6},{9,8},{10,9},{11,10},{13,12},{... | collective-permute-start | bytes 18440 | tf_op jit(solution)/shard_map/ppermute | solution.py:21
  781.7 20.4 %collective-permute-start.3 = (bf16[2,1536]{1,0:T(2,128)(2,1)S(1)}, bf16[2,1536]{1,0:T(2,128)(2,1)S(1)}, u32[]{:S(2)}, u32[]{:S(2)}) collective-permute-start(bf16[2,1536]{1,0:T(2,128)(2,1)S(1)} %get-tuple-element.34), channel_id=1, source_target_pairs={{0,1},{1,2},{2,3},{4,5},{5,6},{6,7},{8,9},{9,10},{10,11},{12,13},{... | collective-permute-start | bytes 18440 | tf_op jit(solution)/shard_map/ppermute | solution.py:20
  810.8 4.6 copy-start.8
  810.8 4.6 copy-start.21
  810.8 4.6 copy-start.23
  810.8 4.6 copy-start.26
  810.8 4.6 copy-start.28
  815.4 59.0 %copy-start.24 = (f32[1280]{0:T(1024)S(1)}, f32[1280]{0:T(1024)}, u32[]{:S(2)}) copy-start(f32[1280]{0:T(1024)} %get-tuple-element.37) | copy-start | bytes 15364
Sparse Core Ops, SparseCore 0:
  9.7 340.7 all-gather.7
  352.1 89.4 all-gather.9
  443.2 87.9 all-gather.11
  605.8 84.7 reduce-scatter.13
  692.8 85.6 reduce-scatter.11
  780.8 328.1 reduce-scatter.9
where the time goes:
time: 1430 us
  blocking collectives  681 us (48%)
  waiting for transfers between devices  397 us (28%)
  local copies, waits for them, and re-layouts  141 us (10%)
  matrix products  131 us (9%)
  other arithmetic  49.5 us (3%)
  between operations  17.1 us (1%)
    psum x1, blocking collectives, sharded_path(): lax.psum((partial_grads[0], partial_grads[1], partial_grads[2], partial_g...  287 us
    unnamed x9, waiting for transfers between devices  229 us
    all_gather x1, waiting for transfers between devices, sharded_path(): lax.all_gather(conv_weight, 'fsdp', axis=2, tiled=True)  114 us
    unnamed x93, local copies, waits for them, and re-layouts  102 us
    psum x1, blocking collectives, on_device(): center_one = lax.psum(jnp.sum(inputs, axis=0), ('seq', 'fsdp')) / total_rows  54.5 us
    all_gather x1, waiting for transfers between devices, sharded_path(): lax.all_gather(pool_weight, 'fsdp', axis=1, tiled=True)  54 us
    psum x1, blocking collectives, on_device(): lax.psum(jnp.sum(jnp.square(inputs - center_one), axis=0), ('seq', 'fsdp'))  52 us
    psum x1, blocking collectives, sharded_path(): center_two = lax.psum(jnp.sum(middle, axis=0), ('seq', 'fsdp')) / total_rows  45.8 us
  transfers between devices with their start and end apart: 10, of which 3 were waited for; matrix products, arithmetic and copies ran while one was open for 16% of the time, Pallas kernels for 0%

commit v1 on v0

v1 whole, which is shorter than its diff:
```python
import functools
import math
import jax
import jax.numpy as jnp
from jax import lax
from jax.experimental import pallas as pl
from jax.experimental.pallas import tpu as pltpu
from jax.sharding import PartitionSpec as P

TRACKS = 5313
WIN = 2048
EPSILON = 1e-05
MESH = pl.DeviceIdType.MESH
BF = jnp.bfloat16
F32 = jnp.float32
GROUP = 8


def dot(a, b, ca, cb):
    return lax.dot_general(a, b, (((ca,), (cb,)), ((), ())), preferred_element_type=F32)


def ds(start, size, step):
    return pl.ds(pl.multiple_of(start, step), size)


def fold(v):
    rows, width = v.shape
    return jnp.sum(v.reshape(rows // 8, 8, width), axis=0)


def rows_loop(total, step, body):
    def run(i, carry):
        body(pl.multiple_of(i * step, step))
        return carry

    lax.fori_loop(0, total // step, run, 0)


def row_sums(total, step, width, count, body):
    def run(i, carry):
        parts = body(pl.multiple_of(i * step, step))
        return tuple(c + fold(v) for c, v in zip(carry, parts))

    zero = tuple(jnp.zeros((8, width), F32) for _ in range(count))
    sums = lax.fori_loop(0, total // step, run, zero)
    return [jnp.sum(v, axis=0, keepdims=True) for v in sums]


def normal(b):
    cdf = 0.5 * (1.0 + lax.erf(b * math.sqrt(0.5)))
    pdf = jnp.exp(-0.5 * b * b) * (1.0 / math.sqrt(2.0 * math.pi))
    return cdf, cdf + b * pdf


class Copy:
    def __init__(self, links, src, there, here, device):
        i = links.count
        links.count += 1
        send, recv = links.send.at[i], links.recv.at[i]

        def make(dst):
            return pltpu.make_async_remote_copy(
                src_ref=src,
                dst_ref=dst,
                send_sem=send,
                recv_sem=recv,
                device_id=device,
                device_id_type=MESH,
            )

        self.links = links
        self.out, self.into = functools.partial(make, there), functools.partial(make, here)

    def start(self):
        self.out().start()
        self.links.started.append(self)
        return self

    def wait_recv(self):
        self.into().wait_recv()

    def wait_send(self):
        self.out().wait_send()


class Links:
    def __init__(self, send, recv):
        self.send, self.recv = send, recv
        self.count = 0
        self.started = []

    def copy(self, src, there, here, device):
        return Copy(self, src, there, here, device)

    def drain(self):
        for item in self.started:
            item.wait_send()
        self.started = []


class Place:
    def __init__(self, seq, fsdp):
        self.seq_size, self.fsdp_size = seq, fsdp
        self.s, self.z = lax.axis_index("seq"), lax.axis_index("fsdp")
        self.part = lax.rem(self.s, GROUP)
        self.base = self.s - self.part

    def near(self, mask):
        return (self.base + jnp.bitwise_xor(self.part, mask), self.z)

    def up(self, d):
        return (self.s, lax.rem(self.z + d, self.fsdp_size))

    def barrier(self):
        bar = pltpu.get_barrier_semaphore()

        def greet(i, carry):
            peer = lax.rem(self.s + i, self.seq_size)
            pl.semaphore_signal(bar, inc=1, device_id=(peer, self.z), device_id_type=MESH)
            return carry

        lax.fori_loop(1, self.seq_size, greet, 0)
        for d in range(1, self.fsdp_size):
            pl.semaphore_signal(bar, inc=1, device_id=self.up(d), device_id_type=MESH)
        pl.semaphore_wait(bar, self.seq_size + self.fsdp_size - 2)


class Exchange:
    def __init__(self, place, mine, seq_slots, fsdp_slots, sems):
        self.place, self.mine = place, mine
        self.seq_slots, self.fsdp_slots = seq_slots, fsdp_slots
        self.seq_send, self.seq_recv, self.fsdp_send, self.fsdp_recv = sems

    def _copy(self, i, stage):
        at = self.place
        if stage == 0:
            peer = lax.rem(at.s + i, at.seq_size)
            source = lax.rem(at.s - i + at.seq_size, at.seq_size)
            device, slots, send, recv, me = (peer, at.z), self.seq_slots, self.seq_send, self.seq_recv, at.s
        else:
            peer = lax.rem(at.z + i, at.fsdp_size)
            source = lax.rem(at.z - i + at.fsdp_size, at.fsdp_size)
            device, slots, send, recv, me = (at.s, peer), self.fsdp_slots, self.fsdp_send, self.fsdp_recv, at.z
        make = lambda slot: pltpu.make_async_remote_copy(
            src_ref=self.mine.at[stage],
            dst_ref=slots.at[slot],
            send_sem=send.at[i],
            recv_sem=recv.at[i],
            device_id=device,
            device_id_type=MESH,
        )
        return functools.partial(make, me), functools.partial(make, source)

    def _each(self, stage, what):
        size = self.place.seq_size if stage == 0 else self.place.fsdp_size

        def run(i, carry):
            what(*self._copy(i, stage))
            return carry

        lax.fori_loop(1, size, run, 0)

    def start(self, block):
        self.mine[0] = block
        self.seq_slots[self.place.s] = block
        self._each(0, lambda out, into: out().start())

    def finish(self, combine):
        self._each(0, lambda out, into: into().wait_recv())
        block = combine(self.seq_slots)
        self.mine[1] = block
        self.fsdp_slots[self.place.z] = block
        self._each(1, lambda out, into: out().start())
        self._each(1, lambda out, into: into().wait_recv())
        block = combine(self.fsdp_slots)
        self._each(0, lambda out, into: out().wait_send())
        self._each(1, lambda out, into: out().wait_send())
        return block


def pack(first, second):
    width = first.shape[1] // 4
    pieces = [v[:, i * width : (i + 1) * width] for v in (first, second) for i in range(4)]
    return jnp.concatenate(pieces, axis=0)


def unpack(block):
    return [jnp.concatenate([block[4 * j + i : 4 * j + i + 1] for i in range(4)], axis=1) for j in range(2)]


def combine_sums(slots):
    return jnp.sum(slots[...], axis=0)


def combine_moments(slots):
    v = slots[...]
    center, spread = v[:, :4], v[:, 4:]
    mean = jnp.mean(center, axis=0)
    rest = jnp.mean(spread + jnp.square(center - mean[None]), axis=0)
    return jnp.concatenate([mean, rest], axis=0)


class Gather:
    def __init__(self, links, at, shard, full):
        self.links, self.at, self.shard, self.full = links, at, shard, full
        rows, self.width = shard.shape
        self.share = rows // GROUP

    def rows(self, part, half=None):
        start = part * self.share
        if half is None:
            return ds(start, self.share, 16)
        return ds(start + half * (self.share // 2), self.share // 2, 16)

    def columns(self, z):
        return ds(z * self.width, self.width, 128)

    def _plane(self, z, mask, of, half=None):
        part = self.at.part
        col = self.columns(z)
        mine = self.full.at[self.rows(jnp.bitwise_xor(part, of), half), col]
        theirs = self.full.at[self.rows(jnp.bitwise_xor(part, of ^ mask), half), col]
        return self.links.copy(mine, mine, theirs, self.at.near(mask)).start()

    def send(self, d):
        at = self.at
        src = self.shard.at[self.rows(at.part)]
        there = self.full.at[self.rows(at.part), self.columns(at.z)]
        source = lax.rem(at.z - d + at.fsdp_size, at.fsdp_size)
        here = self.full.at[self.rows(at.part), self.columns(source)]
        return self.links.copy(src, there, here, at.up(d)).start()

    def run(self, d, first):
        at = self.at
        z = lax.rem(at.z - d + at.fsdp_size, at.fsdp_size)
        held = {}

        def one():
            first[d].wait_recv()
            held["x"] = self._plane(z, 2, 0)
            held["y"] = self._plane(z, 4, 0)
            held["c"] = self._plane(z, 1, 0)
            if d + 1 < at.fsdp_size:
                first[d + 1] = self.send(d + 1)

        def two():
            held["x"].wait_recv()
            held["xa"] = self._plane(z, 4, 2, 0)
            held["xc"] = self._plane(z, 1, 2)

        def three():
            held["y"].wait_recv()
            held["yb"] = self._plane(z, 2, 4, 1)
            held["yc"] = self._plane(z, 1, 4)

        def four():
            held["xa"].wait_recv()
            held["ac"] = self._plane(z, 1, 6, 0)
            held["yb"].wait_recv()
            held["bc"] = self._plane(z, 1, 6, 1)

        def five():
            for name in ("c", "xc", "yc", "ac", "bc"):
                held[name].wait_recv()
            return z

        return one, two, three, four, five


def forward_kernel(
    sizes,
    features,
    conv_shard,
    mix_shard,
    row_pack,
    cotangent,
    scale,
    full_conv,
    full_mix,
    term_mix,
    term_pool,
    pooled,
    active_out,
    middle_low,
    vectors,
    ext,
    taps,
    wbuf,
    mixw,
    middle,
    deriv,
    work,
    a2,
    low,
    low2,
    gbuf,
    pair_one,
    pair_two,
    mine,
    seq_slots,
    fsdp_slots,
    packs,
    send,
    recv,
    seq_send,
    seq_recv,
    fsdp_send,
    fsdp_recv,
    local,
):
    seq, fsdp = sizes
    at = Place(seq, fsdp)
    links = Links(send, recv)
    rows, cin = features.shape
    cout = full_conv.shape[1]
    width = cout // fsdp
    total = float(rows * seq * fsdp)
    taps_count = conv_shard.shape[0] // cin
    lead = 8

    def exchange(i):
        sems = (seq_send.at[i], seq_recv.at[i], fsdp_send.at[i], fsdp_recv.at[i])
        return Exchange(at, mine.at[i], seq_slots.at[i], fsdp_slots.at[i], sems)

    own_conv = pltpu.make_async_copy(conv_shard, full_conv.at[:, ds(at.z * width, width, 128)], local.at[0])
    own_mix = pltpu.make_async_copy(mix_shard, full_mix.at[:, ds(at.z * width, width, 128)], local.at[1])
    own_load = pltpu.make_async_copy(conv_shard, wbuf.at[0], local.at[2])

    at.barrier()
    conv = Gather(links, at, conv_shard, full_conv)
    mix = Gather(links, at, mix_shard, full_mix)
    first_conv, first_mix = {}, {}
    parcels = []
    for d in range(1, fsdp):
        source = lax.rem(at.z - d + fsdp, fsdp)
        parcels.append(links.copy(row_pack, packs.at[at.z], packs.at[source], at.up(d)).start())
    first_conv[1] = conv.send(1)
    own_load.start()
    own_conv.start()
    own_mix.start()
    steps_conv = {d: conv.run(d, first_conv) for d in range(1, fsdp)}
    steps_mix = {d: mix.run(d, first_mix) for d in range(1, fsdp)}

    (sum_one,) = row_sums(rows, 64, cin, 1, lambda r: (features[pl.ds(r, 64), :].astype(F32),))
    mean = sum_one / rows
    (dev_one,) = row_sums(rows, 64, cin, 1, lambda r: (jnp.square(features[pl.ds(r, 64), :].astype(F32) - mean),))
    pad = jnp.zeros((1, cout - cin), F32)
    stats = exchange(0)
    stats.start(pack(jnp.concatenate([mean, pad], axis=1), jnp.concatenate([dev_one / rows, pad], axis=1)))
    packs[at.z] = row_pack[...]
    for parcel in parcels:
        parcel.wait_recv()
    everyone = packs[...].astype(F32)
    params = jnp.sum(everyone[:, :8], axis=0)
    gain_one, shift_one = params[0:1, :cin], params[1:2, :cin]
    gain_two, shift_two, bias_one, bias_two = (params[i : i + 1] for i in range(2, 6))
    mean_one, var_one = unpack(stats.finish(combine_moments))
    mean_one, scale_one = mean_one[:, :cin], lax.rsqrt(var_one[:, :cin] + EPSILON)
    steps_conv[1][0]()

    def active(v):
        b = (v - mean_one) * scale_one * gain_one + shift_one
        return b * (0.5 * (1.0 + lax.erf(b * math.sqrt(0.5))))

    def first_active(r):
        v = active(features[pl.ds(r, 32), :].astype(F32)).astype(BF)
        active_out[pl.ds(r, 32), :] = v
        ext[pl.ds(lead + r, 32), :cin] = v.astype(F32)

    rows_loop(rows, 32, first_active)
    before = packs[lax.rem(at.z + fsdp - 1, fsdp)].astype(F32)[8:16, :cin]
    after = packs[lax.rem(at.z + 1, fsdp)].astype(F32)[8:16, :cin]
    row = lax.broadcasted_iota(jnp.int32, (8, cin), 0)
    ext[0:lead, :cin] = jnp.where((row >= 6) & (at.z > 0), active(before), 0.0)
    ext[lead + rows : lead + rows + 8, :cin] = jnp.where((row < 2) & (at.z < fsdp - 1), active(after), 0.0)
    steps_conv[1][1]()
    steps_conv[1][2]()

    def shifted(k):
        def body(i, carry):
            col = ds(i * 128, 128, 128)
            taps[:, ds(k * cin + i * 128, 128, 128)] = ext[pl.ds(lead - 2 + k, rows), col].astype(BF)
            return carry

        lax.fori_loop(0, cin // 128, body, 0)

    for k in range(taps_count):
        shifted(k)

    def load_block(slot, z):
        copy = pltpu.make_async_copy(full_conv.at[:, ds(z * width, width, 128)], wbuf.at[slot], local.at[3])
        copy.start()
        copy.wait()

    def multiply(slot, z):
        middle[:, ds(z * width, width, 128)] = dot(taps[...], wbuf[slot], 1, 0)

    own_load.wait()
    multiply(0, at.z)
    order = []
    for d in range(1, fsdp):
        one, two, three, four, five = steps_conv[d]
        if d > 1:
            two()
            three()
        four()
        if d + 1 < fsdp:
            steps_conv[d + 1][0]()
        else:
            first_mix[1] = mix.send(1)
        z = five()
        load_block(d % 2, z)
        multiply(d % 2, z)

    steps_mix[1][0]()

    def plus_bias(r):
        v = middle[pl.ds(r, 32), :] + bias_one
        middle[pl.ds(r, 32), :] = v
        return (v,)

    (sum_two,) = row_sums(rows, 32, cout, 1, plus_bias)
    mean = sum_two / rows
    (dev_two,) = row_sums(rows, 32, cout, 1, lambda r: (jnp.square(middle[pl.ds(r, 32), :] - mean),))
    stats = exchange(1)
    stats.start(pack(mean, dev_two / rows))
    steps_mix[1][1]()
    steps_mix[1][2]()
    mean_two, var_two = unpack(stats.finish(combine_moments))
    scale_two = lax.rsqrt(var_two + EPSILON)
    steps_mix[1][3]()
    steps_mix[2][0]()

    def second_active(r):
        b = (middle[pl.ds(r, 32), :] - mean_two) * scale_two * gain_two + shift_two
        cdf, slope = normal(b)
        a2[pl.ds(r, 32), :] = (b * cdf).astype(BF)
        deriv[pl.ds(r, 32), :] = slope

    rows_loop(rows, 32, second_active)
    steps_mix[1][4]()
    for d in range(2, fsdp):
        steps_mix[d][1]()
        steps_mix[d][2]()
        if d + 1 < fsdp:
            steps_mix[d + 1][0]()
        steps_mix[d][3]()
        steps_mix[d][4]()
    own_mix.wait()
    load = pltpu.make_async_copy(full_mix, mixw, local.at[3])
    load.start()
    load.wait()

    tile = 512
    tiles = cout // tile

    def column_loop(body):
        def run(i, carry):
            body(ds(i * tile, tile, 128))
            return carry

        lax.fori_loop(0, tiles, run, 0)

    def add_mix(col):
        work[:, col] = dot(a2[...], mixw[0:cout, col], 1, 0)

    column_loop(add_mix)

    def add_residual(r):
        v = middle[pl.ds(r, 32), :] + work[pl.ds(r, 32), :] + bias_two
        ext[pl.ds(r, 32), :] = v
        low[pl.ds(r, 32), :] = v.astype(BF)

    rows_loop(rows, 32, add_residual)

    def add_pool(col):
        work[:, col] = dot(low[...], mixw[cout : 2 * cout, col], 1, 0)

    column_loop(add_pool)

    def pairs(i, carry):
        col = ds(i * 128, 128, 128)
        even, odd = pl.ds(0, rows // 2, 2), pl.ds(1, rows // 2, 2)
        one, two = pair_one, pair_two
        one[...], two[...] = work[:, col], ext[0:rows, col]
        l0, l1 = one[even, :], one[odd, :]
        s0, s1 = two[even, :], two[odd, :]
        top = jnp.maximum(l0, l1)
        e0, e1 = jnp.exp(l0 - top), jnp.exp(l1 - top)
        inverse = 1.0 / (e0 + e1)
        w0, w1 = e0 * inverse, e1 * inverse
        up = cotangent[:, col].astype(F32) * scale[:, col]
        pooled[:, col] = (w0 * s0 + w1 * s1).astype(BF)
        g0, g1 = s0 * up, s1 * up
        both = w0 * g0 + w1 * g1
        one[even, :] = w0 * up
        one[odd, :] = w1 * up
        two[even, :] = w0 * (g0 - both)
        two[odd, :] = w1 * (g1 - both)
        work[:, col] = one[...]
        low2[:, col] = two[...].astype(BF)
        return carry

    lax.fori_loop(0, cout // 128, pairs, 0)

    def product(left, right):
        def body(i, carry):
            part = ds(i * tile, tile, 128)
            gbuf[part, :] = dot(left[:, part], right[...], 0, 0).astype(BF)
            return carry

        lax.fori_loop(0, tiles, body, 0)

    product(low, low2)
    out_pool = pltpu.make_async_copy(gbuf, term_pool, local.at[4])
    out_pool.start()

    def back_pool(col):
        ext[0:rows, col] = dot(low2[...], mixw[ds(cout + col.start, tile, 128), :], 1, 1)

    column_loop(back_pool)

    def grad_summed(r):
        v = work[pl.ds(r, 32), :] + ext[pl.ds(r, 32), :]
        work[pl.ds(r, 32), :] = v
        low[pl.ds(r, 32), :] = v.astype(BF)
        return (v,)

    (sum_bias_two,) = row_sums(rows, 32, cout, 1, grad_summed)

    def back_mix(col):
        ext[0:rows, col] = dot(low[...], mixw[ds(col.start, tile, 128), :], 1, 1)

    column_loop(back_mix)

    def normed(r):
        return (middle[pl.ds(r, 32), :] - mean_two) * scale_two

    def grad_before(r):
        v = ext[pl.ds(r, 32), :] * deriv[pl.ds(r, 32), :]
        ext[pl.ds(r, 32), :] = v
        return v, v * normed(r)

    sum_shift, sum_gain = row_sums(rows, 32, cout, 2, grad_before)
    stats = exchange(2)
    stats.start(pack(sum_shift, sum_gain))
    out_pool.wait()
    product(a2, low)
    out_mix = pltpu.make_async_copy(gbuf, term_mix, local.at[4])
    out_mix.start()
    shift_two_grad, gain_two_grad = unpack(stats.finish(combine_sums))

    def grad_middle(r):
        v = work[pl.ds(r, 32), :] + gain_two * scale_two * (
            ext[pl.ds(r, 32), :] - shift_two_grad / total - normed(r) * gain_two_grad / total
        )
        middle_low[pl.ds(r, 32), :] = v.astype(BF)
        return (v,)

    (sum_bias_one,) = row_sums(rows, 32, cout, 1, grad_middle)
    fill = lambda v: jnp.concatenate([v, pad], axis=1)
    vectors[0:8, :] = jnp.concatenate(
        [fill(mean_one), fill(scale_one), fill(gain_one), fill(shift_one), shift_two_grad, gain_two_grad, sum_bias_one, sum_bias_two],
        axis=0,
    )
    own_conv.wait()
    out_mix.wait()
    links.drain()


def run_forward(sizes, features, conv_shard, mix_shard, row_pack, cotangent, scale):
    seq, fsdp = sizes
    rows, cin = features.shape
    cout = conv_shard.shape[1] * fsdp
    deep = conv_shard.shape[0]
    two = mix_shard.shape[0]
    shape = jax.ShapeDtypeStruct
    vmem = pl.BlockSpec(memory_space=pltpu.VMEM)
    hbm = pl.BlockSpec(memory_space=pl.ANY)
    copies = 80
    return pl.pallas_call(
        functools.partial(forward_kernel, sizes),
        out_shape=(
            shape((deep, cout), BF),
            shape((two, cout), BF),
            shape((cout, cout), BF),
            shape((cout, cout), BF),
            shape((rows // 2, cout), BF),
            shape((rows, cin), BF),
            shape((rows, cout), BF),
            shape((8, cout), F32),
        ),
        in_specs=[vmem, hbm, hbm, vmem, vmem, vmem],
        out_specs=(hbm, hbm, hbm, hbm, vmem, vmem, vmem, vmem),
        scratch_shapes=[
            pltpu.VMEM((rows + 16, cout), F32),
            pltpu.VMEM((rows, deep), BF),
            pltpu.VMEM((2, deep, cout // fsdp), BF),
            pltpu.VMEM((two, cout), BF),
            pltpu.VMEM((rows, cout), F32),
            pltpu.VMEM((rows, cout), F32),
            pltpu.VMEM((rows, cout), F32),
            pltpu.VMEM((rows, cout), BF),
            pltpu.VMEM((rows, cout), BF),
            pltpu.VMEM((rows, cout), BF),
            pltpu.VMEM((cout, cout), BF),
            pltpu.VMEM((rows, 128), F32),
            pltpu.VMEM((rows, 128), F32),
            pltpu.VMEM((3, 2, 8, cout // 4), F32),
            pltpu.VMEM((3, seq, 8, cout // 4), F32),
            pltpu.VMEM((3, fsdp, 8, cout // 4), F32),
            pltpu.VMEM((fsdp, 16, cout), BF),
            pltpu.SemaphoreType.DMA((copies,)),
            pltpu.SemaphoreType.DMA((copies,)),
            pltpu.SemaphoreType.DMA((3, seq)),
            pltpu.SemaphoreType.DMA((3, seq)),
            pltpu.SemaphoreType.DMA((3, fsdp)),
            pltpu.SemaphoreType.DMA((3, fsdp)),
            pltpu.SemaphoreType.DMA((5,)),
        ],
        compiler_params=pltpu.CompilerParams(
            collective_id=0, has_side_effects=True, vmem_limit_bytes=62 * 2**20
        ),
    )(features, conv_shard, mix_shard, row_pack, cotangent, scale)


def parameter_pack(owner, features, first, second):
    cout = second[0].shape[0] * lax.axis_size("fsdp")
    out = jnp.zeros((16, cout), BF)
    block = jnp.stack(first)
    out = lax.dynamic_update_slice(out, block, (0, owner * block.shape[1]))
    block = jnp.stack(second)
    out = lax.dynamic_update_slice(out, block, (2, owner * block.shape[1]))
    rows, cin = features.shape
    out = out.at[8:10, :cin].set(features[0:2])
    return out.at[14:16, :cin].set(features[rows - 2 : rows])


def spread_sum(v):
    size = lax.axis_size("seq")
    bit = GROUP
    while bit < size:
        v = v + lax.ppermute(v, "seq", [(i, i ^ bit) for i in range(size)])
        bit *= 2
    return v


def extended(shard, axis, width):
    size, length = lax.axis_size(axis), shard.shape[0]
    up = [(i, (i + 1) % size) for i in range(size - 1)]
    down = [(j, i) for i, j in up]
    before = lax.ppermute(shard[length - width :], axis, up)
    after = lax.ppermute(shard[:width], axis, down)
    return jnp.concatenate([before, shard, after], axis=0)


def on_device(
    features,
    conv_weight,
    mix_weight,
    pool_weight,
    gain_first,
    shift_first,
    gain_second,
    shift_second,
    bias_conv,
    bias_mix,
    cotangent,
    track_counts,
):
    rows, cin = features.shape
    seq, fsdp = lax.axis_size("seq"), lax.axis_size("fsdp")
    total = float(rows * seq * fsdp)
    position = lax.axis_index(("seq", "fsdp"))
    owner = lax.axis_index("fsdp")
    window = position * rows // WIN
    width = conv_weight.shape[2]
    cout = width * fsdp
    taps = conv_weight.shape[0]
    scale = lax.dynamic_slice_in_dim(track_counts, window, 1).astype(F32) / TRACKS
    scale = jnp.broadcast_to(scale[:, None], (1, cout))
    row_pack = parameter_pack(
        owner, features, (gain_first, shift_first), (gain_second, shift_second, bias_conv, bias_mix)
    )
    full_conv, full_mix, term_mix, term_pool, pooled, active_one, middle_low, vectors = run_forward(
        (seq, fsdp),
        features,
        conv_weight.reshape(taps * cin, width),
        jnp.concatenate([mix_weight, pool_weight], axis=0),
        row_pack,
        cotangent,
        scale,
    )
    mean_one, scale_one, gain_one, shift_one = (vectors[i, :cin] for i in range(4))
    shift_two_grad, gain_two_grad, sum_bias_one, sum_bias_two = (vectors[i] for i in range(4, 8))
    normed_one = (features.astype(F32) - mean_one) * scale_one
    before_one = normed_one * gain_one + shift_one

    padded_one = extended(active_one, "fsdp", 2)
    padded_grad = extended(middle_low, "fsdp", 2)
    full_conv = full_conv.reshape(taps, cin, cout)
    term_conv = []
    grad_active = 0.0
    for k in range(taps):
        term_conv.append(
            jnp.einsum("pc,pd->cd", padded_one[k : k + rows], middle_low, preferred_element_type=F32).astype(BF)
        )
        begin = taps - 1 - k
        grad_active = grad_active + jnp.einsum(
            "pd,cd->pc", padded_grad[begin : begin + rows], full_conv[k], preferred_element_type=F32
        )
    def reduced(v):
        out = lax.psum_scatter(v, "fsdp", scatter_dimension=v.ndim - 1, tiled=True)
        out = lax.psum_scatter(out, "seq", scatter_dimension=v.ndim - 2, tiled=True)
        return lax.all_gather(out, "seq", axis=v.ndim - 2, tiled=True).astype(F32)

    grad_conv = reduced(jnp.stack(term_conv))
    grad_mix, grad_pool = reduced(term_mix), reduced(term_pool)
    cdf, slope = normal(before_one)
    grad_before = slope * grad_active
    sums = lax.psum(
        (jnp.sum(grad_before, axis=0), jnp.sum(grad_before * normed_one, axis=0), sum_bias_one, sum_bias_two),
        ("seq", "fsdp"),
    )
    shift_one_grad, gain_one_grad, bias_one_grad, bias_two_grad = sums
    grad_features = (
        gain_one * scale_one * (grad_before - shift_one_grad / total - normed_one * gain_one_grad / total)
    ).astype(BF)

    def share(v, size):
        return lax.dynamic_slice_in_dim(v, owner * size, size)

    first, second = gain_first.shape[0], gain_second.shape[0]
    return (
        pooled,
        grad_features,
        grad_conv,
        grad_mix,
        grad_pool,
        share(gain_one_grad, first),
        share(shift_one_grad, first),
        share(gain_two_grad, second),
        share(shift_two_grad, second),
        share(bias_one_grad, second),
        share(bias_two_grad, second),
    )


def solution(mesh):
    rows = P(("seq", "fsdp"), None)
    vector = P("fsdp")
    in_specs = (rows, P(None, None, "fsdp"), P(None, "fsdp"), P(None, "fsdp")) + (vector,) * 6 + (rows, P())
    out_specs = (rows, rows, P(None, None, "fsdp"), P(None, "fsdp"), P(None, "fsdp")) + (vector,) * 6
    return jax.shard_map(on_device, mesh=mesh, in_specs=in_specs, out_specs=out_specs, check_vma=False)
```

time: 1430 us -> 1060 us (0.74)
  blocking collectives: 681 us -> 39.9 us
  Pallas kernels: 0 us -> 266 us
  waiting for transfers between devices: 397 us -> 531 us
  matrix products: 131 us -> 46.9 us
  other arithmetic: 49.5 us -> 19.5 us
  local copies, waits for them, and re-layouts: 141 us -> 114 us
    psum x7 -> x1, blocking collectives: 570 us -> 39.9 us  [on_device(): lax.psum((jnp.sum(grad_before, axis=0), jnp.sum(grad_before * normed_one,...]
    pallas_call x0 -> x1, Pallas kernels: none -> 266 us  [run_forward(): pl.pallas_call(functools.partial(forward_kernel, sizes), out_shape=(shape...]
    unnamed x9 -> x12, waiting for transfers between devices: 229 us -> 401 us
    all_gather x3, waiting for transfers between devices: 168 us -> 9.81 us  [reduced(): return lax.all_gather(out, 'seq', axis=v.ndim - 2, tiled=True).astype(F32)]
    reduce_scatter x0 -> x3, waiting for transfers between devices: none -> 119 us  [reduced(): out = lax.psum_scatter(out, 'seq', scatter_dimension=v.ndim - 2, tiled=True)]
    all_gather x4 -> x0, blocking collectives: 86 us -> none  [the longest x1 36.8 us: sharded_path(): lax.all_gather(shift_second, 'fsdp', axis=0, tiled=True)]
    dot_general x21 -> x10, matrix products: 131 us -> 46.9 us  [the longest x5 26.2 us: on_device(): jnp.einsum('pd,cd->pc', padded_grad[begin:begin + rows], full_conv[k], pr...]
    unnamed x2 -> x0, blocking collectives: 25 us -> none
  transfers between devices with their start and end apart: 10 -> 13, of which waited for: 3 -> 7; matrix products, arithmetic and copies ran while one was open for 16% -> 15% of each run, Pallas kernels for 0% -> 0%
where the time goes in v1:
time: 1060 us; the launch traced here: 1040 us
  waiting for transfers between devices  531 us (50%)
  Pallas kernels  266 us (25%)
  local copies, waits for them, and re-layouts  114 us (11%)
  matrix products  46.9 us (4%)
  blocking collectives  39.9 us (4%)
  other arithmetic  19.5 us (2%)
  between operations  15 us (1%)
  starting transfers between devices  12 us (1%)
    unnamed x12, waiting for transfers between devices  401 us
    pallas_call x1, Pallas kernels, run_forward(): pl.pallas_call(functools.partial(forward_kernel, sizes), out_shape=(shape...  266 us
    reduce_scatter x3, waiting for transfers between devices, reduced(): out = lax.psum_scatter(out, 'seq', scatter_dimension=v.ndim - 2, tiled=True)  119 us
    unnamed x25, local copies, waits for them, and re-layouts  102 us
    psum x1, blocking collectives, on_device(): lax.psum((jnp.sum(grad_before, axis=0), jnp.sum(grad_before * normed_one,...  39.9 us
    dot_general x5, matrix products, on_device(): jnp.einsum('pd,cd->pc', padded_grad[begin:begin + rows], full_conv[k], pr...  26.2 us
  transfers between devices with their start and end apart: 13, of which 7 were waited for; matrix products, arithmetic and copies ran while one was open for 15% of the time, Pallas kernels for 0%

profile of v1, /device:TPU:0, one launch (start us, length us, event | category | flops | bytes accessed | tf_op | source)
XLA Modules:
  0.0 1044.6 jit_solution(14995901584505001301)
XLA Ops:
  7.2 1.2 dynamic_slice.25
  9.1 0.7 stack.42
  9.8 0.7 stack.43
  10.5 0.7 stack.45
  11.2 0.7 stack.46
  11.9 0.7 stack.47
  12.6 0.7 stack.48
  14.3 0.7 slice_dynamic-update-slice_fusion.1
  15.0 0.7 slice_dynamic-update-slice_fusion.row_pack
  15.8 3.3 pad_maximum_fusion.mix_shard
  19.7 265.8 %shard_map.203 = (bf16[6400,1536]{1,0:T(8,128)(2,1)}, bf16[3072,1536]{1,0:T(8,128)(2,1)}, bf16[1536,1536]{1,0:T(8,128)(2,1)}, bf16[1536,1536]{1,0:T(8,128)(2,1)}...) custom-call(bf16[512,1280]{1,0:T(8,128)(2,1)} %features.1, ...), custom_call_target="tpu_custom_call" | custom-call | tf_op jit(solution)/shard_map/pallas_call | solution.py:582
  285.5 6.6 copy.25
  292.2 6.9 copy.27
  299.1 1.2 copy-done.2
  300.3 1.3 collective-permute-start.3
  301.6 4.5 collective-permute-start.2
  306.3 1.2 collective-permute-done.2
  307.5 4.2 fusion.1
  311.8 4.1 fusion.3
  315.9 4.1 fusion.5
  320.0 4.1 fusion.7
  324.1 4.1 fusion.9
  328.2 37.5 %copy.23 = bf16[5,1280,1536]{1,0,2:T(8,128)(2,1)} copy(bf16[5,1280,1536]{2,1,0:T(8,128)(2,1)} %fusion.9) | data formatting | bytes 39321600
  365.7 22.7 %copy.29 = bf16[192,8,5,1280]{3,1,2,0:T(8,128)(2,1)} copy(bf16[192,8,5,1280]{3,2,1,0:T(8,128)(2,1)} %bitcast.37) | data formatting | bytes 39321600
  388.6 2.4 copy.26
  391.0 74.0 %reduce-scatter.23.cloned.1.call-done = bf16[384,1536]{1,0:T(8,128)(2,1)} async-done(((bf16[1536,1536]{1,0:T(8,128)(2,1)}), bf16[384,1536]{1,0:T(8,128)(2,1)}) %reduce-scatter.23.cloned.1.call-update) | async-done | bytes 1179664
  465.0 2.4 copy.28
  467.4 326.8 %reduce-scatter.19.cloned.1.call-done = bf16[384,6400]{1,0:T(8,128)(2,1)} async-done(((bf16[1536,6400]{1,0:T(8,128)(2,1)}), bf16[384,6400]{1,0:T(8,128)(2,1)}) %reduce-scatter.19.cloned.1.call-update) | async-done | bytes 4915216
  794.3 11.9 %reshape.108 = bf16[384,5,1280]{2,1,0:T(8,128)(2,1)} reshape(bf16[384,6400]{1,0:T(8,128)(2,1)} %reduce-scatter.19.cloned.1.call-done) | data formatting | bytes 9830400
  806.2 9.8 copy.24
  816.0 20.3 %reduce-scatter.15.cloned.1.call-done = bf16[192,384]{1,0:T(8,128)(2,1)} async-done(((bf16[1536,384]{1,0:T(8,128)(2,1)}), bf16[192,384]{1,0:T(8,128)(2,1)}) %reduce-scatter.15.cloned.1.call-update) | async-done | bytes 147472 | tf_op jit(solution)/shard_map/reduce_scatter | solution.py:715
  836.4 40.4 %reduce-scatter.17.cloned.1.call-done = bf16[192,384]{1,0:T(8,128)(2,1)} async-done(((bf16[1536,384]{1,0:T(8,128)(2,1)}), bf16[192,384]{1,0:T(8,128)(2,1)}) %reduce-scatter.17.cloned.1.call-update) | async-done | bytes 147472 | tf_op jit(solution)/shard_map/reduce_scatter | solution.py:715
  876.8 58.6 %reduce-scatter.13.cloned.1.call-done = bf16[5,160,384]{2,1,0:T(8,128)(2,1)} async-done(((bf16[5,1280,384]{2,1,0:T(8,128)(2,1)}), bf16[5,160,384]{2,1,0:T(8,128)(2,1)}) %reduce-scatter.13.cloned.1.call-update) | async-done | bytes 614416 | tf_op jit(solution)/shard_map/reduce_scatter | solution.py:715
  935.4 1.3 collective-permute-start
  936.7 4.5 collective-permute-start.1
  941.5 5.8 fusion.14
  948.0 4.4 fusion.10
  952.4 4.4 fusion.12
  956.8 4.5 fusion.16
  961.3 7.2 fusion.53
  968.5 39.9 %all-reduce = (f32[1280]{0:T(1024)S(1)}, f32[1280]{0:T(1024)S(1)}, f32[1536]{0:T(1024)S(1)}, f32[1536]{0:T(1024)S(1)}) all-reduce(f32[1280]{0:T(1024)S(1)} %get-tuple-element.50, f32[1280]{0:T(1024)S(1)} %get-tuple-element.49, f32[1536]{0:T(1024)S(1)} %get-tuple-element.52, ...), channel_id=1, replica_groups=mesh['seq'=8,'fsdp'=4] {'seq','fsdp'}, use_global_device_ids=true, to_apply=%region_3.4 | all-reduce | flops 5632 | bytes 45056 | tf_op jit(solution)/shard_map/psum | solution.py:722
  1008.4 0.7 dynamic_slice.32
  1011.0 3.5 multiply_convert_fusion
  1014.5 2.8 convert_element_type.42
  1017.3 2.8 convert_element_type.43
  1020.2 9.8 all-gather.4.cloned.1.call-done
  1030.0 7.0 convert_element_type.41
  1036.9 0.9 copy.41
  (56 shorter events, 5.1 us)
Async XLA Ops:
  7.2 381.4 %reduce-scatter.21.cloned.1.call-start = ((), (), s32[]{:S(2)}) async-start(), calls=%async_computation.13 | async-start | bytes 5898240
  15.8 3.9 copy-start.4
  292.1 172.9 %reduce-scatter.23.cloned.1.call-start = ((), (), s32[]{:S(2)}) async-start(), calls=%async_computation.14 | async-start | bytes 5898240
  299.0 1.3 copy-start.2
  299.0 8.5 copy-start.1
  299.0 495.2 %reduce-scatter.19.cloned.1.call-start = ((), (), s32[]{:S(2)}) async-start(), calls=%async_computation.12 | async-start | bytes 24576000
  300.3 6.0 collective-permute-start.3
  301.6 5.9 collective-permute-start.2
  388.5 447.8 %reduce-scatter.15.cloned.1.call-start = ((), (), s32[]{:S(2)}) async-start(), calls=%async_computation.8 | async-start | bytes 1327104 | tf_op jit(solution)/shard_map/reduce_scatter | solution.py:715
  391.0 485.8 %reduce-scatter.17.cloned.1.call-start = ((), (), s32[]{:S(2)}) async-start(), calls=%async_computation.10 | async-start | bytes 1327104 | tf_op jit(solution)/shard_map/reduce_scatter | solution.py:715
  467.4 468.0 %reduce-scatter.13.cloned.1.call-start = ((), (), s32[]{:S(2)}) async-start(), calls=%async_computation.6 | async-start | bytes 5529600 | tf_op jit(solution)/shard_map/reduce_scatter | solution.py:715
  815.9 125.4 %copy-start.5 = (f32[8,1536]{1,0:T(8,128)S(1)}, f32[8,1536]{1,0:T(8,128)}, u32[]{:S(2)}) copy-start(f32[8,1536]{1,0:T(8,128)} %get-tuple-element.43) | copy-start | bytes 147460
  816.0 198.5 %all-gather.6.cloned.1.call-start = ((), (), s32[]{:S(2)}) async-start(), calls=%async_computation.9 | async-start | bytes 1327104 | tf_op jit(solution)/shard_map/all_gather | solution.py:716
  836.3 181.0 %all-gather.8.cloned.1.call-start = ((), (), s32[]{:S(2)}) async-start(), calls=%async_computation.11 | async-start | bytes 1327104 | tf_op jit(solution)/shard_map/all_gather | solution.py:716
  876.8 153.2 %all-gather.4.cloned.1.call-start = ((), (), s32[]{:S(2)}) async-start(), calls=%async_computation.7 | async-start | bytes 5529600 | tf_op jit(solution)/shard_map/all_gather | solution.py:716
  935.4 12.5 %collective-permute-start = (bf16[2,1536]{1,0:T(2,128)(2,1)S(1)}, bf16[2,1536]{1,0:T(2,128)(2,1)S(1)}, u32[]{:S(2)}, u32[]{:S(2)}) collective-permute-start(bf16[2,1536]{1,0:T(2,128)(2,1)S(1)} %get-tuple-element.62), channel_id=1, source_target_pairs={{1,0},{2,1},{3,2},{5,4},{6,5},{7,6},{9,8},{10,9},{11,10},{13,12},{... | collective-permute-start | bytes 18440 | tf_op jit(solution)/shard_map/ppermute | solution.py:654
  936.7 11.3 %collective-permute-start.1 = (bf16[2,1536]{1,0:T(2,128)(2,1)S(1)}, bf16[2,1536]{1,0:T(2,128)(2,1)S(1)}, u32[]{:S(2)}, u32[]{:S(2)}) collective-permute-start(bf16[2,1536]{1,0:T(2,128)(2,1)S(1)} %get-tuple-element.63), channel_id=1, source_target_pairs={{0,1},{1,2},{2,3},{4,5},{5,6},{6,7},{8,9},{9,10},{10,11},{12,13},{... | collective-permute-start | bytes 18440 | tf_op jit(solution)/shard_map/ppermute | solution.py:653
  956.7 4.6 copy-start
  956.8 4.6 copy-start.6
  1020.2 16.8 %copy-start.3 = (bf16[256,1536]{1,0:T(8,128)(2,1)S(1)}, bf16[256,1536]{1,0:T(8,128)(2,1)}, u32[]{:S(2)}) copy-start(bf16[256,1536]{1,0:T(8,128)(2,1)} %get-tuple-element.82) | copy-start | bytes 2359300
Sparse Core Ops, SparseCore 0:
  292.2 84.6 reduce-scatter.20
  379.2 85.7 reduce-scatter.22
  467.4 326.8 reduce-scatter.18
  798.3 37.9 reduce-scatter.14
  840.0 36.7 reduce-scatter.16
  880.5 54.8 reduce-scatter.12
  937.3 24.0 all-gather.5
  963.3 24.4 all-gather.7
  989.7 40.2 all-gather.3

commit v2 on v1

--- a/solution.py
+++ b/solution.py
@@ -166,27 +166,34 @@
         self.seq_slots[self.place.s] = block
         self._each(0, lambda out, into: out().start())
 
-    def finish(self, combine):
+    def middle(self, combine):
         self._each(0, lambda out, into: into().wait_recv())
         block = combine(self.seq_slots)
         self.mine[1] = block
         self.fsdp_slots[self.place.z] = block
         self._each(1, lambda out, into: out().start())
+
+    def end(self, combine):
         self._each(1, lambda out, into: into().wait_recv())
         block = combine(self.fsdp_slots)
         self._each(0, lambda out, into: out().wait_send())
         self._each(1, lambda out, into: out().wait_send())
         return block
 
-
-def pack(first, second):
-    width = first.shape[1] // 4
-    pieces = [v[:, i * width : (i + 1) * width] for v in (first, second) for i in range(4)]
+    def finish(self, combine):
+        self.middle(combine)
+        return self.end(combine)
+
+
+def pack(*vectors):
+    width = vectors[0].shape[1] // 4
+    pieces = [v[:, i * width : (i + 1) * width] for v in vectors for i in range(4)]
     return jnp.concatenate(pieces, axis=0)
 
 
 def unpack(block):
-    return [jnp.concatenate([block[4 * j + i : 4 * j + i + 1] for i in range(4)], axis=1) for j in range(2)]
+    count = block.shape[0] // 4
+    return [jnp.concatenate([block[4 * j + i : 4 * j + i + 1] for i in range(4)], axis=1) for j in range(count)]
 
 
 def combine_sums(slots):
@@ -201,6 +208,42 @@
     return jnp.concatenate([mean, rest], axis=0)
 
 
+class Spread:
+    def __init__(self, links, at, place, source=None):
+        self.links, self.at, self.place, self.source = links, at, place, source
+        self.held = {}
+
+    def _send(self, name, mask, of, half=None):
+        part = self.at.part
+        mine = self.place(jnp.bitwise_xor(part, of), half)
+        theirs = self.place(jnp.bitwise_xor(part, of ^ mask), half)
+        src = mine if of or self.source is None else self.source
+        self.held[name] = self.links.copy(src, mine, theirs, self.at.near(mask)).start()
+
+    def one(self):
+        self._send("x", 2, 0)
+        self._send("y", 4, 0)
+        self._send("c", 1, 0)
+
+    def two(self):
+        self.held["x"].wait_recv()
+        self._send("xa", 4, 2, 0)
+        self._send("xc", 1, 2)
+        self.held["y"].wait_recv()
+        self._send("yb", 2, 4, 1)
+        self._send("yc", 1, 4)
+
+    def three(self):
+        self.held["xa"].wait_recv()
+        self._send("ac", 1, 6, 0)
+        self.held["yb"].wait_recv()
+        self._send("bc", 1, 6, 1)
+
+    def four(self):
+        for name in ("c", "xc", "yc", "ac", "bc"):
+            self.held[name].wait_recv()
+
+
 class Gather:
     def __init__(self, links, at, shard, full):
         self.links, self.at, self.shard, self.full = links, at, shard, full
@@ -215,13 +258,6 @@
 
     def columns(self, z):
         return ds(z * self.width, self.width, 128)
-
-    def _plane(self, z, mask, of, half=None):
-        part = self.at.part
-        col = self.columns(z)
-        mine = self.full.at[self.rows(jnp.bitwise_xor(part, of), half), col]
-        theirs = self.full.at[self.rows(jnp.bitwise_xor(part, of ^ mask), half), col]
-        return self.links.copy(mine, mine, theirs, self.at.near(mask)).start()
 
     def send(self, d):
         at = self.at
@@ -234,38 +270,28 @@
     def run(self, d, first):
         at = self.at
         z = lax.rem(at.z - d + at.fsdp_size, at.fsdp_size)
-        held = {}
+        spread = Spread(self.links, at, lambda part, half: self.full.at[self.rows(part, half), self.columns(z)])
 
         def one():
             first[d].wait_recv()
-            held["x"] = self._plane(z, 2, 0)
-            held["y"] = self._plane(z, 4, 0)
-            held["c"] = self._plane(z, 1, 0)
+            spread.one()
             if d + 1 < at.fsdp_size:
                 first[d + 1] = self.send(d + 1)
 
-        def two():
-            held["x"].wait_recv()
-            held["xa"] = self._plane(z, 4, 2, 0)
-            held["xc"] = self._plane(z, 1, 2)
-
-        def three():
-            held["y"].wait_recv()
-            held["yb"] = self._plane(z, 2, 4, 1)
-            held["yc"] = self._plane(z, 1, 4)
-
         def four():
-            held["xa"].wait_recv()
-            held["ac"] = self._plane(z, 1, 6, 0)
-            held["yb"].wait_recv()
-            held["bc"] = self._plane(z, 1, 6, 1)
-
-        def five():
-            for name in ("c", "xc", "yc", "ac", "bc"):
-                held[name].wait_recv()
+            spread.four()
             return z
 
-        return one, two, three, four, five
+        return one, spread.two, lambda: None, spread.three, four
+
+
+def put_blocks(target, half, values, col):
+    size = values.shape[0] // 8
+    for i in range(8):
+        part, side = 4 * half + i // 2, i % 2
+        c, x, y = part & 1, part >> 1 & 1, part >> 2
+        at = 8 * c + 4 * side + (2 * x + y if side == 0 else 2 * y + x)
+        target[at * size : (at + 1) * size, col] = values[i * size : (i + 1) * size].astype(BF)
 
 
 def forward_kernel(
@@ -323,8 +349,8 @@
         sems = (seq_send.at[i], seq_recv.at[i], fsdp_send.at[i], fsdp_recv.at[i])
         return Exchange(at, mine.at[i], seq_slots.at[i], fsdp_slots.at[i], sems)
 
-    own_conv = pltpu.make_async_copy(conv_shard, full_conv.at[:, ds(at.z * width, width, 128)], local.at[0])
-    own_mix = pltpu.make_async_copy(mix_shard, full_mix.at[:, ds(at.z * width, width, 128)], local.at[1])
+    own_conv = pltpu.make_async_copy(wbuf.at[0], full_conv.at[:, ds(at.z * width, width, 128)], local.at[0])
+    own_mix = pltpu.make_async_copy(mix_shard, mixw.at[:, ds(at.z * width, width, 128)], local.at[1])
     own_load = pltpu.make_async_copy(conv_shard, wbuf.at[0], local.at[2])
 
     at.barrier()
@@ -337,7 +363,6 @@
         parcels.append(links.copy(row_pack, packs.at[at.z], packs.at[source], at.up(d)).start())
     first_conv[1] = conv.send(1)
     own_load.start()
-    own_conv.start()
     own_mix.start()
     steps_conv = {d: conv.run(d, first_conv) for d in range(1, fsdp)}
     steps_mix = {d: mix.run(d, first_mix) for d in range(1, fsdp)}
@@ -397,7 +422,9 @@
         middle[:, ds(z * width, width, 128)] = dot(taps[...], wbuf[slot], 1, 0)
 
     own_load.wait()
+    own_conv.start()
     multiply(0, at.z)
+    own_conv.wait()
     order = []
     for d in range(1, fsdp):
         one, two, three, four, five = steps_conv[d]
@@ -448,9 +475,11 @@
         steps_mix[d][3]()
         steps_mix[d][4]()
     own_mix.wait()
-    load = pltpu.make_async_copy(full_mix, mixw, local.at[3])
-    load.start()
-    load.wait()
+    for d in range(1, fsdp):
+        col = ds(lax.rem(at.z + d, fsdp) * width, width, 128)
+        load = pltpu.make_async_copy(full_mix.at[:, col], mixw.at[:, col], local.at[3])
+        load.start()
+        load.wait()
 
     tile = 512
     tiles = cout // tile
@@ -505,12 +534,14 @@
     lax.fori_loop(0, cout // 128, pairs, 0)
 
     def product(left, right):
-        def body(i, carry):
-            part = ds(i * tile, tile, 128)
-            gbuf[part, :] = dot(left[:, part], right[...], 0, 0).astype(BF)
-            return carry
-
-        lax.fori_loop(0, tiles, body, 0)
+        half = cout // 2
+        for i in range(2):
+            def body(j, carry):
+                col = ds(j * tile, tile, 128)
+                put_blocks(gbuf, i, dot(left[:, i * half : (i + 1) * half], right[:, col], 0, 0), col)
+                return carry
+
+            lax.fori_loop(0, tiles, body, 0)
 
     product(low, low2)
     out_pool = pltpu.make_async_copy(gbuf, term_pool, local.at[4])
@@ -564,7 +595,6 @@
         [fill(mean_one), fill(scale_one), fill(gain_one), fill(shift_one), shift_two_grad, gain_two_grad, sum_bias_one, sum_bias_two],
         axis=0,
     )
-    own_conv.wait()
     out_mix.wait()
     links.drain()
 
@@ -625,6 +655,359 @@
     )(features, conv_shard, mix_shard, row_pack, cotangent, scale)
 
 
+class Reduce:
+    def __init__(self, links, at, unit, first, slot, buffers, core_slot, credit):
+        self.links, self.at, self.unit, self.slot = links, at, unit, slot
+        self.core_slot, self.credit = core_slot, credit
+        self.from_x, self.from_y, self.from_yx, self.from_xy, self.own, self.from_z, self.total = (
+            buffers[0].at[pl.ds(2 * first, 2 * unit)],
+            buffers[1].at[pl.ds(2 * first, 2 * unit)],
+            buffers[2].at[pl.ds(first, unit)],
+            buffers[3].at[pl.ds(first, unit)],
+            buffers[4].at[pl.ds(2 * first, 2 * unit)],
+            buffers[5].at[:, pl.ds(2 * first, 2 * unit)],
+            buffers[6].at[pl.ds(2 * first, 2 * unit)],
+        )
+        part = at.part
+        self.c, self.x, self.y = part & 1, (part >> 1) & 1, part >> 2
+        self.sent = []
+
+    def _rows(self, start, count):
+        return self.slot.at[ds(start * self.unit, count * self.unit, 16)]
+
+    def _send(self, src, dst, device):
+        copy = self.links.copy(src, dst, dst, device).start()
+        self.links.started.remove(copy)
+        self.sent.append(copy)
+        return copy
+
+    def core(self, wait_credit):
+        if wait_credit:
+            pl.semaphore_wait(self.credit, 1)
+        dst = self.core_slot.at[pl.ds(0, 8 * self.unit)]
+        self.by_core = self._send(self._rows((1 - self.c) * 8, 8), dst, self.at.near(1))
+
+    def _add(self, start, other, count, out=None):
+        step = 16
+        mine = self._rows(start, count)
+        out = mine if out is None else out
+
+        def body(r):
+            v = mine[pl.ds(r, step), :].astype(F32) + other[pl.ds(r, step), :].astype(F32)
+            out[pl.ds(r, step), :] = v.astype(BF)
+
+        rows_loop(count * self.unit, step, body)
+
+    def plane(self, give_credit):
+        self.by_core.wait_recv()
+        self._add(self.c * 8, self.core_slot, 8)
+        if give_credit:
+            pl.semaphore_signal(self.credit, inc=1, device_id=self.at.near(1), device_id_type=MESH)
+        self.a, self.b = self.c * 8, self.c * 8 + 4
+        self.by_x = self._send(self._rows(self.a + (1 - self.x) * 2, 2), self.from_x, self.at.near(2))
+        self.by_y = self._send(self._rows(self.b + (1 - self.y) * 2, 2), self.from_y, self.at.near(4))
+
+    def cross(self):
+        a, b = self.a + self.x * 2, self.b + self.y * 2
+        self.by_x.wait_recv()
+        self._add(a, self.from_x, 2)
+        self.by_yx = self._send(self._rows(a + 1 - self.y, 1), self.from_yx, self.at.near(4))
+        self.by_y.wait_recv()
+        self._add(b, self.from_y, 2)
+        self.by_xy = self._send(self._rows(b + 1 - self.x, 1), self.from_xy, self.at.near(2))
+        self.a, self.b = a + self.y, b + self.x
+
+    def depth(self):
+        self.by_yx.wait_recv()
+        self._add(self.a, self.from_yx, 1, self.own.at[pl.ds(0, self.unit)])
+        self.by_xy.wait_recv()
+        self._add(self.b, self.from_xy, 1, self.own.at[pl.ds(self.unit, self.unit)])
+        width = self.total.shape[1]
+        at = self.at
+        self.by_z = []
+        for d in range(1, at.fsdp_size):
+            col = ds(lax.rem(at.z + d, at.fsdp_size) * width, width, 128)
+            dst = self.from_z.at[d - 1]
+            self.by_z.append(self.links.copy(self.own.at[:, col], dst, dst, at.up(d)).start())
+
+    def finish(self):
+        width = self.total.shape[1]
+        col = ds(self.at.z * width, width, 128)
+        for copy in self.by_z:
+            copy.wait_recv()
+
+        def body(r):
+            v = self.own[pl.ds(r, 16), col].astype(F32)
+            for d in range(self.at.fsdp_size - 1):
+                v = v + self.from_z[d, pl.ds(r, 16), :].astype(F32)
+            self.total[pl.ds(r, 16), :] = v.astype(BF)
+
+        rows_loop(2 * self.unit, 16, body)
+
+    def free(self):
+        for copy in self.sent:
+            copy.wait_send()
+        self.sent = []
+
+
+def backward_kernel(
+    sizes,
+    features,
+    active_one,
+    middle_low,
+    vectors,
+    full_conv,
+    term_mix,
+    term_pool,
+    gathered,
+    grad_features,
+    sums_out,
+    ext,
+    shifted,
+    weight,
+    grad_active,
+    slots,
+    core_slots,
+    from_x,
+    from_y,
+    from_yx,
+    from_xy,
+    own,
+    from_z,
+    total,
+    edges,
+    mine,
+    seq_slots,
+    fsdp_slots,
+    send,
+    recv,
+    seq_send,
+    seq_recv,
+    fsdp_send,
+    fsdp_recv,
+    credits,
+    local,
+):
+    seq, fsdp = sizes
+    at = Place(seq, fsdp)
+    links = Links(send, recv)
+    rows, cin = features.shape
+    cout = full_conv.shape[1]
+    taps = full_conv.shape[0] // cin
+    all_rows = float(rows * seq * fsdp)
+    lead = 8
+    buffers = (from_x, from_y, from_yx, from_xy, own, from_z, total)
+    heights = [cout, cout] + [cin] * taps
+    chunks, first = [], 0
+    for i, height in enumerate(heights):
+        unit = height // 16
+        chunks.append(
+            Reduce(links, at, unit, first, slots.at[i % 3], buffers, core_slots.at[i % 2], credits.at[i % 2])
+        )
+        first += unit
+    share = 2 * first
+    count = len(chunks)
+
+    def load_weight(k):
+        return pltpu.make_async_copy(full_conv.at[pl.ds(k * cin, cin)], weight.at[k % 2], local.at[k % 2])
+
+    load_weight(0).start()
+    loads = []
+    for i, term in enumerate((term_pool, term_mix)):
+        loads.append(pltpu.make_async_copy(term, slots.at[i], local.at[2 + i]))
+        loads[i].start()
+    at.barrier()
+    below = links.copy(middle_low.at[pl.ds(0, 16)], edges.at[1], edges.at[1], at.up(fsdp - 1)).start()
+    above = links.copy(middle_low.at[pl.ds(rows - 16, 16)], edges.at[0], edges.at[0], at.up(1)).start()
+
+    def core(i):
+        chunks[i].core(i >= 2)
+
+    def plane(i):
+        chunks[i].plane(i + 2 < count)
+
+    for i in range(2):
+        loads[i].wait()
+        core(i)
+
+    def widen(r):
+        ext[pl.ds(lead + r, 32), :] = middle_low[pl.ds(r, 32), :].astype(F32)
+
+    rows_loop(rows, 32, widen)
+    below.wait_recv()
+    above.wait_recv()
+    ext[0:lead, :] = jnp.where(at.z > 0, edges[0].astype(F32)[8:16], 0.0)
+    ext[lead + rows : lead + rows + 8, :] = jnp.where(at.z < fsdp - 1, edges[1].astype(F32)[0:8], 0.0)
+    half_width = (taps - 1) // 2
+    tile = 512
+
+    def shift(k):
+        start = lead + half_width - k
+
+        def body(i, carry):
+            col = ds(i * 128, 128, 128)
+            shifted[:, col] = ext[pl.ds(start, rows), col].astype(BF)
+            return carry
+
+        lax.fori_loop(0, cout // 128, body, 0)
+
+    def product(slot):
+        half = cin // 2
+        for i in range(2):
+
+            def body(j, carry):
+                col = ds(j * tile, tile, 128)
+                put_blocks(slot, i, dot(active_one[:, i * half : (i + 1) * half], shifted[:, col], 0, 0), col)
+                return carry
+
+            lax.fori_loop(0, cout // tile, body, 0)
+
+    def back(k):
+        load_weight(k).wait()
+        if k + 1 < taps:
+            load_weight(k + 1).start()
+
+        def body(j, carry):
+            col = ds(j * 256, 256, 128)
+            v = dot(shifted[...], weight[k % 2, col, :], 1, 1)
+            grad_active[:, col] = v if k == 0 else grad_active[:, col] + v
+            return carry
+
+        lax.fori_loop(0, cin // 256, body, 0)
+
+    groups = {}
+
+    def spread(lo, hi):
+        start = 2 * sum(c.unit for c in chunks[:lo])
+        size = 2 * sum(c.unit for c in chunks[lo:hi])
+
+        def place(part, half):
+            if half is None:
+                return gathered.at[ds(part * share + start, size, 16)]
+            return gathered.at[ds(part * share + start + half * (size // 2), size // 2, 16)]
+
+        groups[lo] = Spread(links, at, place, total.at[pl.ds(start, size)])
+        groups[lo].one()
+
+    plane(0)
+    for k in range(taps):
+        i = k + 2
+        shift(k)
+        if i >= 3:
+            chunks[i - 3].depth()
+            chunks[i - 3].free()
+        product(slots.at[i % 3])
+        core(i)
+        plane(i - 1)
+        chunks[i - 2].cross()
+        back(k)
+        if i >= 4:
+            chunks[i - 4].finish()
+        if i == 5:
+            spread(0, 2)
+
+    mean_one, scale_one, gain_one, shift_one = (vectors[i : i + 1, :cin] for i in range(4))
+
+    def grad_before(r):
+        normed = (features[pl.ds(r, 32), :].astype(F32) - mean_one) * scale_one
+        v = normal(normed * gain_one + shift_one)[1] * grad_active[pl.ds(r, 32), :]
+        grad_active[pl.ds(r, 32), :] = v
+        return v, v * normed
+
+    sum_shift, sum_gain = row_sums(rows, 32, cin, 2, grad_before)
+    pad = jnp.zeros((1, cout - cin), F32)
+    wide = lambda v: jnp.concatenate([v, pad], axis=1)
+    sems = (seq_send, seq_recv, fsdp_send, fsdp_recv)
+    stats = Exchange(at, mine, seq_slots, fsdp_slots, sems)
+    stats.start(pack(wide(sum_shift), wide(sum_gain), vectors[6:7, :], vectors[7:8, :]))
+    plane(count - 1)
+    chunks[count - 2].cross()
+    stats.middle(combine_sums)
+    groups[0].two()
+    chunks[count - 3].depth()
+    chunks[count - 4].finish()
+    chunks[count - 1].cross()
+    spread(2, count - 3)
+    groups[0].three()
+    chunks[count - 2].depth()
+    chunks[count - 3].finish()
+    everyone = unpack(stats.end(combine_sums))
+    shift_grad, gain_grad = everyone[0][:, :cin], everyone[1][:, :cin]
+
+    def store(r):
+        normed = (features[pl.ds(r, 32), :].astype(F32) - mean_one) * scale_one
+        v = grad_active[pl.ds(r, 32), :] - shift_grad / all_rows - normed * gain_grad / all_rows
+        grad_features[pl.ds(r, 32), :] = (gain_one * scale_one * v).astype(BF)
+
+    rows_loop(rows, 32, store)
+    sums_out[0:4, :] = jnp.concatenate(everyone, axis=0)
+    chunks[count - 1].depth()
+    groups[2].two()
+    chunks[count - 2].finish()
+    groups[2].three()
+    chunks[count - 1].finish()
+    spread(count - 3, count)
+    keep = pltpu.make_async_copy(total, gathered.at[ds(at.part * share, share, 16)], local.at[4])
+    keep.start()
+    groups[0].four()
+    groups[2].four()
+    groups[count - 3].two()
+    groups[count - 3].three()
+    groups[count - 3].four()
+    keep.wait()
+    for chunk in chunks:
+        chunk.free()
+    links.drain()
+
+
+def run_backward(sizes, features, active_one, middle_low, vectors, full_conv, term_mix, term_pool):
+    seq, fsdp = sizes
+    rows, cin = features.shape
+    deep, cout = full_conv.shape
+    width = cout // fsdp
+    share = (deep + 2 * cout) // GROUP
+    shape = jax.ShapeDtypeStruct
+    vmem = pl.BlockSpec(memory_space=pltpu.VMEM)
+    hbm = pl.BlockSpec(memory_space=pl.ANY)
+    copies = 160
+    return pl.pallas_call(
+        functools.partial(backward_kernel, sizes),
+        out_shape=(shape((GROUP * share, width), BF), shape((rows, cin), BF), shape((8, cout), F32)),
+        in_specs=[vmem, vmem, vmem, vmem, hbm, hbm, hbm],
+        out_specs=(hbm, vmem, vmem),
+        scratch_shapes=[
+            pltpu.VMEM((rows + 16, cout), F32),
+            pltpu.VMEM((rows, cout), BF),
+            pltpu.VMEM((2, cin, cout), BF),
+            pltpu.VMEM((rows, cin), F32),
+            pltpu.VMEM((3, cout, cout), BF),
+            pltpu.VMEM((2, cout // 2, cout), BF),
+            pltpu.VMEM((share, cout), BF),
+            pltpu.VMEM((share, cout), BF),
+            pltpu.VMEM((share // 2, cout), BF),
+            pltpu.VMEM((share // 2, cout), BF),
+            pltpu.VMEM((share, cout), BF),
+            pltpu.VMEM((fsdp - 1, share, width), BF),
+            pltpu.VMEM((share, width), BF),
+            pltpu.VMEM((2, 16, cout), BF),
+            pltpu.VMEM((2, 16, cout // 4), F32),
+            pltpu.VMEM((seq, 16, cout // 4), F32),
+            pltpu.VMEM((fsdp, 16, cout // 4), F32),
+            pltpu.SemaphoreType.DMA((copies,)),
+            pltpu.SemaphoreType.DMA((copies,)),
+            pltpu.SemaphoreType.DMA((seq,)),
+            pltpu.SemaphoreType.DMA((seq,)),
+            pltpu.SemaphoreType.DMA((fsdp,)),
+            pltpu.SemaphoreType.DMA((fsdp,)),
+            pltpu.SemaphoreType.REGULAR((2,)),
+            pltpu.SemaphoreType.DMA((5,)),
+        ],
+        compiler_params=pltpu.CompilerParams(
+            collective_id=1, has_side_effects=True, vmem_limit_bytes=62 * 2**20
+        ),
+    )(features, active_one, middle_low, vectors, full_conv, term_mix, term_pool)
+
+
 def parameter_pack(owner, features, first, second):
     cout = second[0].shape[0] * lax.axis_size("fsdp")
     out = jnp.zeros((16, cout), BF)
@@ -644,15 +1027,6 @@
         v = v + lax.ppermute(v, "seq", [(i, i ^ bit) for i in range(size)])
         bit *= 2
     return v
-
-
-def extended(shard, axis, width):
-    size, length = lax.axis_size(axis), shard.shape[0]
-    up = [(i, (i + 1) % size) for i in range(size - 1)]
-    down = [(j, i) for i, j in up]
-    before = lax.ppermute(shard[length - width :], axis, up)
-    after = lax.ppermute(shard[:width], axis, down)
-    return jnp.concatenate([before, shard, after], axis=0)
 
 
 def on_device(
@@ -671,7 +1045,6 @@
 ):
     rows, cin = features.shape
     seq, fsdp = lax.axis_size("seq"), lax.axis_size("fsdp")
-    total = float(rows * seq * fsdp)
     position = lax.axis_index(("seq", "fsdp"))
     owner = lax.axis_index("fsdp")
     window = position * rows // WIN
@@ -692,41 +1065,20 @@
         cotangent,
         scale,
     )
-    mean_one, scale_one, gain_one, shift_one = (vectors[i, :cin] for i in range(4))
-    shift_two_grad, gain_two_grad, sum_bias_one, sum_bias_two = (vectors[i] for i in range(4, 8))
-    normed_one = (features.astype(F32) - mean_one) * scale_one
-    before_one = normed_one * gain_one + shift_one
-
-    padded_one = extended(active_one, "fsdp", 2)
-    padded_grad = extended(middle_low, "fsdp", 2)
-    full_conv = full_conv.reshape(taps, cin, cout)
-    term_conv = []
-    grad_active = 0.0
-    for k in range(taps):
-        term_conv.append(
-            jnp.einsum("pc,pd->cd", padded_one[k : k + rows], middle_low, preferred_element_type=F32).astype(BF)
-        )
-        begin = taps - 1 - k
-        grad_active = grad_active + jnp.einsum(
-            "pd,cd->pc", padded_grad[begin : begin + rows], full_conv[k], preferred_element_type=F32
-        )
-    def reduced(v):
-        out = lax.psum_scatter(v, "fsdp", scatter_dimension=v.ndim - 1, tiled=True)
-        out = lax.psum_scatter(out, "seq", scatter_dimension=v.ndim - 2, tiled=True)
-        return lax.all_gather(out, "seq", axis=v.ndim - 2, tiled=True).astype(F32)
-
-    grad_conv = reduced(jnp.stack(term_conv))
-    grad_mix, grad_pool = reduced(term_mix), reduced(term_pool)
-    cdf, slope = normal(before_one)
-    grad_before = slope * grad_active
-    sums = lax.psum(
-        (jnp.sum(grad_before, axis=0), jnp.sum(grad_before * normed_one, axis=0), sum_bias_one, sum_bias_two),
-        ("seq", "fsdp"),
+    gathered, grad_features, sums = run_backward(
+        (seq, fsdp), features, active_one, middle_low, vectors, full_conv, term_mix, term_pool
     )
-    shift_one_grad, gain_one_grad, bias_one_grad, bias_two_grad = sums
-    grad_features = (
-        gain_one * scale_one * (grad_before - shift_one_grad / total - normed_one * gain_one_grad / total)
-    ).astype(BF)
+    parts = spread_sum(gathered.reshape(GROUP, -1, width).astype(F32))
+    taken = 0
+    products = []
+    for height in [cout, cout] + [cin] * taps:
+        size = height // GROUP
+        products.append(parts[:, taken : taken + size].reshape(height, width))
+        taken += size
+    grad_pool, grad_mix = products[:2]
+    grad_conv = jnp.stack(products[2:])
+    shift_two_grad, gain_two_grad = vectors[4], vectors[5]
+    shift_one_grad, gain_one_grad, bias_one_grad, bias_two_grad = sums[0], sums[1], sums[2], sums[3]
 
     def share(v, size):
         return lax.dynamic_slice_in_dim(v, owner * size, size)

time: 1060 us -> 412 us (0.39); the launches traced: 1040 us -> 410 us
  waiting for transfers between devices: 531 us -> 0 us
  Pallas kernels: 266 us -> 381 us
  local copies, waits for them, and re-layouts: 114 us -> 24.5 us
  matrix products: 46.9 us -> 0 us
  blocking collectives: 39.9 us -> 0 us
  other arithmetic: 19.5 us -> 3.31 us
  between operations: 15 us -> 1.44 us
  starting transfers between devices: 12 us -> 0 us
    unnamed x12 -> x0, waiting for transfers between devices: 401 us -> none
    pallas_call x0 -> x1, Pallas kernels: none -> 190 us  [run_backward(): pl.pallas_call(functools.partial(backward_kernel, sizes), out_shape=(shap...]
    reduce_scatter x3 -> x0, waiting for transfers between devices: 119 us -> none  [reduced(): out = lax.psum_scatter(out, 'seq', scatter_dimension=v.ndim - 2, tiled=True)]
    unnamed x25 -> x16, local copies, waits for them, and re-layouts: 102 us -> 6.56 us
    pallas_call x1, Pallas kernels: 266 us -> 191 us  [run_forward(): pl.pallas_call(functools.partial(forward_kernel, sizes), out_shape=(shape...]
    dot_general x10 -> x0, matrix products: 46.9 us -> none  [the longest x5 26.2 us: on_device(): jnp.einsum('pd,cd->pc', padded_grad[begin:begin + rows], full_conv[k], pr...]
    psum x1 -> x0, blocking collectives: 39.9 us -> none  [on_device(): lax.psum((jnp.sum(grad_before, axis=0), jnp.sum(grad_before * normed_one,...]
    convert_element_type x4 -> x0, other arithmetic: 16.1 us -> none  [the longest x3 12.6 us: reduced(): return lax.all_gather(out, 'seq', axis=v.ndim - 2, tiled=True).astype(F32)]
  transfers between devices with their start and end apart: 13 -> 0, of which waited for: 7 -> 0; matrix products, arithmetic and copies ran while one was open for 15% -> 0% of each run, Pallas kernels for 0% -> 0%
where the time goes in v2:
time: 412 us; the launch traced here: 410 us
  Pallas kernels  381 us (92%)
  local copies, waits for them, and re-layouts  24.5 us (6%)
    pallas_call x1, Pallas kernels, run_forward(): pl.pallas_call(functools.partial(forward_kernel, sizes), out_shape=(shape...  191 us
    pallas_call x1, Pallas kernels, run_backward(): pl.pallas_call(functools.partial(backward_kernel, sizes), out_shape=(shap...  190 us

profile of v2, /device:TPU:0, one launch (start us, length us, event | category | flops | bytes accessed | tf_op | source)
XLA Modules:
  0.0 410.4 jit_solution(13798831160905280054)
XLA Ops:
  0.7 1.2 dynamic_slice.33
  2.6 0.7 stack.27
  3.2 0.7 stack.28
  3.9 0.7 stack.30
  4.6 0.7 stack.31
  5.3 0.7 stack.32
  6.0 0.7 stack.33
  6.7 0.6 broadcast_in_dim.13.scale
  7.3 0.4 dynamic_update_slice.6
  7.7 0.5 dynamic_update_slice.7
  8.2 0.7 slice_dynamic-update-slice_fusion.1
  9.0 0.7 slice_dynamic-update-slice_fusion.row_pack
  9.7 0.0 copy-start.4
  9.7 3.3 pad_maximum_fusion.mix_shard
  13.0 0.0 copy-done.4
  13.0 191.4 %shard_map.203 = (bf16[6400,1536]{1,0:T(8,128)(2,1)}, bf16[3072,1536]{1,0:T(8,128)(2,1)}, bf16[1536,1536]{1,0:T(8,128)(2,1)}, bf16[1536,1536]{1,0:T(8,128)(2,1)}...) custom-call(bf16[512,1280]{1,0:T(8,128)(2,1)} %features.3, ...), custom_call_target="tpu_custom_call" | custom-call | tf_op jit(solution)/shard_map/pallas_call | solution.py:612
  204.5 0.9 fusion.9
  205.4 189.7 %shard_map.204 = (bf16[9472,384]{1,0:T(8,128)(2,1)}, bf16[512,1280]{1,0:T(8,128)(2,1)}, f32[8,1536]{1,0:T(8,128)}) custom-call(bf16[512,1280]{1,0:T(8,128)(2,1)} %features.3, bf16[512,1280]{1,0:T(8,128)(2,1)} %get-tuple-element.46.active_one, bf16[512,1536]{1,0:T(8,128)(2,1)} %get-tuple-element.47.middle_low, f32[8,1536]{1,0:T(8,128)} %get-tuple-element.48.vectors, ...), custom_call_target="tpu_custom_call" | custom-call | tf_op jit(solution)/shard_map/pallas_call | solution.py:973
  395.1 0.6 fusion.2
  395.7 1.0 fusion.8
  396.6 0.6 fusion.4
  397.2 0.7 fusion
  397.9 0.0 copy-start
  397.9 4.4 %fusion.6 = (f32[8,192,384]{2,1,0:T(8,128)}, f32[8,192,384]{2,1,0:T(8,128)}) fusion(bf16[8,1184,384]{2,1,0:T(8,128)(2,1)} %bitcast.21), kind=kLoop, calls=%fused_computation.22 | loop fusion | bytes 9437184 | tf_op jit(solution)/shard_map/slice | solution.py:1076
  402.4 0.6 copy-done
  402.9 1.2 fusion.7
  404.2 0.1 bitcast_dynamic-update-slice_fusion.4
  404.3 0.1 bitcast_dynamic-update-slice_fusion.3
  404.4 0.1 bitcast_dynamic-update-slice_fusion.2
  404.6 0.1 bitcast_dynamic-update-slice_fusion.1
  404.7 0.0 copy-start.2
  404.7 0.0 copy-start.1
  404.7 0.1 bitcast_dynamic-update-slice_fusion
  404.9 1.0 copy-done.2
  405.8 0.0 copy-start.3
  405.9 0.9 copy.33
  406.7 0.0 copy-done.1
  406.8 1.5 copy.34
  408.2 2.1 copy-done.3
  (3 shorter events, 0.0 us)
Async XLA Ops:
  9.7 3.3 copy-start.4
  397.9 5.0 %copy-start = (bf16[9472,384]{1,0:T(8,128)(2,1)S(1)}, bf16[9472,384]{1,0:T(8,128)(2,1)}, u32[]{:S(2)}) copy-start(bf16[9472,384]{1,0:T(8,128)(2,1)} %get-tuple-element.53) | copy-start | bytes 21823492
  404.7 1.1 copy-start.2
  404.7 2.0 copy-start.1
  405.8 4.5 %copy-start.3 = (f32[5,1280,384]{2,1,0:T(8,128)}, f32[5,1280,384]{2,1,0:T(8,128)S(1)}, u32[]{:S(2)}) copy-start(f32[5,1280,384]{2,1,0:T(8,128)S(1)} %bitcast_dynamic-update-slice_fusion) | copy-start | bytes 29491204
